TPU v7x, 1024 devices: a whole 4x4x32 slice. The times are simulated.
1024 devices in a mesh: dp: 16 (over x, y), fsdp: 64 (over z, core).
Axes of the slice: x: 4, y: 4, z: 32, core: 2. Of those that a mesh axis runs over, the one named last changes fastest.
Arguments:
- grad: bfloat16 [64, 16, 4, 16384], P('fsdp', 'dp'), may hold values from -19 to 19
- block_owner: int32 [256], replicated, may hold values from 0 to 63, as said below
- left: float32 [64, 4, 8, 16, 4, 512], P('fsdp', None, None, 'dp'), may hold values from -6 to 6
- right: float32 [64, 4, 8, 16, 4, 512], P('fsdp', None, None, 'dp'), may hold values from -6 to 6
- left_root: bfloat16 [64, 4, 8, 16, 4, 512], P('fsdp', None, None, 'dp'), may hold values from -0.125 to 4.625
- right_root: bfloat16 [64, 4, 8, 16, 4, 512], P('fsdp', None, None, 'dp'), may hold values from -0.125 to 1.625
- moment: float32 [64, 4, 8, 16, 4, 512], P('fsdp', None, None, 'dp'), may hold values from 0.05 to 2
Outputs:
- update: bfloat16 [64, 16, 4, 16384], P('fsdp', 'dp')
- left_new: float32 [64, 4, 8, 16, 4, 512], P('fsdp', None, None, 'dp')
- right_new: float32 [64, 4, 8, 16, 4, 512], P('fsdp', None, None, 'dp')
- moment_new: float32 [64, 4, 8, 16, 4, 512], P('fsdp', None, None, 'dp')
Inputs may be any that keep to these rules, and one draw needn't show every extreme that they name: `block_owner`: each of the 64 owners holds exactly 4 blocks and at most 1 block of one band; every owner of a band holds exactly 1 of its blocks.
All inputs are finite; a program needn't handle non-finite values.
Results may differ from a plain program's by a relative error of at most 0.0049.
Values may be sent and summed in bfloat16 or wider, within the bound.
No kernel may reach another device: no remote copies, remote signals or barrier semaphores. Data moves between devices by JAX's collectives and lax.ppermute only.
A program may use at most 128 MiB of HBM per device.

v0:
```python
import jax
import jax.numpy as jnp
from jax import lax
from jax.sharding import PartitionSpec as P

FACTOR_DECAY = 0.999
MOMENT_DECAY = 0.95
ADAM_EPS = 1e-08
NORM_EPS = 1e-06


def block_tables(block_owner, col_blocks, owners, slot_count):
    total_blocks = block_owner.shape[0]
    block_ids = jnp.arange(total_blocks, dtype=jnp.int32)
    earlier = block_ids[None, :] < block_ids[:, None]
    same_owner = block_owner[None, :] == block_owner[:, None]
    band_of = block_ids // col_blocks
    same_band = band_of[None, :] == band_of[:, None]
    slot_rank = jnp.sum(jnp.logical_and(same_owner, earlier).astype(jnp.int32), axis=1)
    placing = jnp.sum((same_owner & same_band & earlier).astype(jnp.int32), axis=1)
    slot_table = (
        jnp.zeros((owners, slot_count), jnp.int32).at[block_owner, slot_rank].set(block_ids)
    )
    return (slot_table, placing)


def body(grad, block_owner, left, right, left_root, right_root, moment):
    replicas = lax.axis_size("dp")
    owners = lax.axis_size("fsdp")
    my_replica = lax.axis_index("dp")
    my_owner = lax.axis_index("fsdp")
    dev_rows = grad.shape[2]
    columns_all = grad.shape[3]
    slot_count = left.shape[1]
    band_shards = left.shape[2]
    width = left.shape[5]
    col_blocks = columns_all // width
    per_band = min(owners, col_blocks)
    capacity = col_blocks // per_band
    mine_rows = band_shards * dev_rows
    slot_table, placing = block_tables(block_owner, col_blocks, owners, slot_count)
    my_band = my_owner // band_shards
    band_owner = lax.dynamic_slice_in_dim(block_owner, my_band * col_blocks, col_blocks)
    band_place = lax.dynamic_slice_in_dim(placing, my_band * col_blocks, col_blocks)
    target = band_owner * capacity + band_place
    selector = (target[None, :] == jnp.arange(owners * capacity, dtype=jnp.int32)[:, None]).astype(
        jnp.bfloat16
    )
    pieces = grad.reshape(dev_rows, col_blocks, width)
    outgoing = jnp.einsum(
        "rc,icj->rij", selector, pieces, preferred_element_type=jnp.float32
    ).astype(jnp.bfloat16)
    outgoing = outgoing.reshape(owners, capacity, dev_rows, width)
    arrived = lax.all_to_all(outgoing, "fsdp", split_axis=0, concat_axis=0, tiled=True)
    owned_ids = lax.dynamic_slice_in_dim(slot_table, my_owner, 1, 0).reshape(slot_count)
    owned_band = owned_ids // col_blocks
    owned_place = placing[owned_ids]
    sources = owned_band[:, None] * band_shards + jnp.arange(band_shards, dtype=jnp.int32)[None, :]
    gathered_rows = arrived[sources, owned_place[:, None]]
    own_grad = gathered_rows.reshape(slot_count, mine_rows, width)
    own_values = own_grad.astype(jnp.float32)
    moment_new = (
        MOMENT_DECAY * moment.reshape(slot_count, mine_rows, width)
        + (1.0 - MOMENT_DECAY) * own_values * own_values
    )
    adam_step = own_values / (jnp.sqrt(moment_new) + ADAM_EPS)
    adam_sq = jnp.sum(adam_step * adam_step, axis=(1, 2))
    left_rows = left_root.reshape(slot_count, mine_rows, width)
    shaped = own_grad.reshape(1, slot_count, band_shards, 1, dev_rows, width)
    full_grad, full_root = (
        lax.all_gather(shaped, "dp", axis=3, tiled=True),
        lax.all_gather(right_root, "dp", axis=3, tiled=True),
    )
    full_grad = full_grad.reshape(slot_count, width, width)
    full_root = full_root.reshape(slot_count, width, width)
    left_gram = jnp.einsum("kra,kba->krb", own_grad, full_grad, preferred_element_type=jnp.float32)
    my_cols = lax.dynamic_slice_in_dim(
        full_grad.reshape(slot_count, width, band_shards, replicas, dev_rows), my_replica, 1, 3
    )
    my_cols = my_cols.reshape(slot_count, width, mine_rows)
    right_gram = jnp.einsum("kam,kab->kmb", my_cols, full_grad, preferred_element_type=jnp.float32)
    left_mixed = jnp.einsum(
        "kra,kab->krb", left_rows, full_grad, preferred_element_type=jnp.float32
    ).astype(jnp.bfloat16)
    precond = jnp.einsum("kra,kab->krb", left_mixed, full_root, preferred_element_type=jnp.float32)
    left_new = (
        FACTOR_DECAY * left.reshape(slot_count, mine_rows, width) + (1.0 - FACTOR_DECAY) * left_gram
    )
    right_new = (
        FACTOR_DECAY * right.reshape(slot_count, mine_rows, width)
        + (1.0 - FACTOR_DECAY) * right_gram
    )
    precond_sq = jnp.sum(precond * precond, axis=(1, 2))
    adam_total, precond_total = lax.psum((adam_sq, precond_sq), "dp")
    graft_scale = jnp.sqrt(adam_total) / jnp.sqrt(precond_total + NORM_EPS)
    update_rows = (precond * graft_scale[:, None, None]).astype(jnp.bfloat16)
    returning = jnp.zeros((owners, capacity, dev_rows, width), jnp.bfloat16)
    returning = returning.at[sources, owned_place[:, None]].set(
        update_rows.reshape(slot_count, band_shards, dev_rows, width)
    )
    returned = lax.all_to_all(returning, "fsdp", split_axis=0, concat_axis=0, tiled=True)
    flat_back = returned.reshape(owners * capacity, dev_rows, width)
    assembled = jnp.einsum(
        "rc,rij->icj", selector, flat_back, preferred_element_type=jnp.float32
    ).astype(jnp.bfloat16)
    update = assembled.reshape(grad.shape)
    return (
        update,
        left_new.reshape(left.shape),
        right_new.reshape(right.shape),
        moment_new.reshape(moment.shape),
    )


def solution(mesh):
    placed = (
        P("fsdp", "dp", None, None),
        P(),
        P("fsdp", None, None, "dp", None, None),
        P("fsdp", None, None, "dp", None, None),
        P("fsdp", None, None, "dp", None, None),
        P("fsdp", None, None, "dp", None, None),
        P("fsdp", None, None, "dp", None, None),
    )
    return jax.shard_map(
        body,
        mesh=mesh,
        in_specs=placed,
        out_specs=(
            P("fsdp", "dp", None, None),
            P("fsdp", None, None, "dp", None, None),
            P("fsdp", None, None, "dp", None, None),
            P("fsdp", None, None, "dp", None, None),
        ),
        check_vma=False,
    )
```

profile of v0, /device:TPU:1, one launch (start us, length us, event | category | flops | bytes accessed | tf_op | source)
XLA Modules:
  0.0 310.5 jit_solution(17038338146599608994)
XLA Ops:
  7.2 0.7 all-gather.4.cloned.1.call-update
  7.9 1.0 convert_reduce_fusion
  8.9 0.8 dynamic-slice_add_fusion
  9.7 1.2 fusion.2
  10.9 0.9 copy.55
  11.9 30.5 %all-to-all-start = ((bf16[64,1,4,512]{3,2,1,0:T(4,128)(2,1)}), bf16[64,1,4,512]{3,2,1,0:T(4,128)(2,1)S(1)}, u32[]{:S(2)}, u32[]{:S(2)}) async-start(bf16[64,1,4,512]{3,2,1,0:T(4,128)(2,1)} %copy.55), calls=%async_computation | async-start | bytes 524288 | tf_op jit(solution)/shard_map/all_to_all | solution.py:54
  42.4 0.7 compare_select_fusion.2
  43.2 11.3 %scatter_fusion = s32[64,4]{0,1:T(4,128)S(1)} fusion(s32[64,4]{0,1:T(4,128)S(1)} %broadcast_in_dim.9, s32[256]{0:T(256)S(1)} %bitcast.62, s32[256]{0:T(256)S(1)} %iota.25), kind=kCustom, calls=%fused_computation.2 | custom fusion | bytes 5120 | tf_op jit(solution)/shard_map/scatter | solution.py:22
  54.7 0.6 gather_fusion
  55.5 28.1 %all-to-all-done = bf16[64,1,4,512]{3,2,1,0:T(4,128)(2,1)S(1)} async-done(((bf16[64,1,4,512]{3,2,1,0:T(4,128)(2,1)}), bf16[64,1,4,512]{3,2,1,0:T(4,128)(2,1)S(1)}, u32[]{:S(2)}, u32[]{:S(2)}) %all-to-all-start) | async-done | bytes 262176 | tf_op jit(solution)/shard_map/all_to_all | solution.py:54
  83.7 0.7 gather_fusion.1
  84.4 0.7 copy.85
  85.5 17.7 %all-gather.4.cloned.1.call-done = bf16[1,4,8,16,4,512]{5,4,3,2,1,0:T(4,128)(2,1)} async-done(((bf16[1,4,8,1,4,512]{5,4,3,2,1,0:T(4,128)(2,1)}), bf16[1,4,8,16,4,512]{5,4,3,2,1,0:T(4,128)(2,1)}) %all-gather.4.cloned.1.call-update) | async-done | bytes 2097168 | tf_op jit(solution)/shard_map/all_gather | solution.py:72
  103.2 4.0 %reshape.228 = bf16[4,512,512]{2,1,0:T(8,128)(2,1)} reshape(bf16[1,4,8,16,4,512]{5,4,3,2,1,0:T(4,128)(2,1)} %all-gather.4.cloned.1.call-done) | data formatting | bytes 4194304 | tf_op jit(solution)/shard_map/reshape | solution.py:75
  107.2 81.3 %all-gather.6.cloned.1.call-done = bf16[4,8,64,512]{3,1,0,2:T(8,128)(2,1)} async-done(((bf16[4,8,4,512]{3,1,0,2:T(8,128)(2,1)}), bf16[4,8,64,512]{3,1,0,2:T(8,128)(2,1)}) %all-gather.6.cloned.1.call-update) | async-done | bytes 2097168 | tf_op jit(solution)/shard_map/all_gather | solution.py:71
  188.4 2.7 copy.57
  191.2 2.5 multiply_reduce_fusion
  193.7 31.0 %all-reduce = (f32[4]{0:T(128)S(1)}, f32[4]{0:T(128)S(1)}) all-reduce(f32[4]{0:T(128)S(1)} %get-tuple-element.34, f32[4]{0:T(128)S(1)} %fusion.13), channel_id=1, replica_groups=mesh['dp'=16,'fsdp'=64] {'dp'}, use_global_device_ids=true, to_apply=%region_6.7 | all-reduce | flops 8 | bytes 64 | tf_op jit(solution)/shard_map/psum | solution.py:94
  224.9 0.8 broadcast.271
  225.6 4.0 %scatter_fusion.1 = bf16[64,4,512]{2,1,0:T(4,128)(2,1)} fusion(bf16[64,4,512]{2,1,0:T(4,128)(2,1)} %broadcast.271, s32[32]{0:T(128)S(1)} %reshape.260, bf16[32,4,512]{2,1,0:T(4,128)(2,1)S(1)} %reshape.262), kind=kCustom, calls=%fused_computation.3 | custom fusion | bytes 393344 | tf_op jit(solution)/shard_map/scatter | solution.py:98
  229.7 31.7 %all-to-all-start.1 = ((bf16[64,1,4,512]{3,2,1,0:T(4,128)(2,1)}), bf16[64,1,4,512]{3,2,1,0:T(4,128)(2,1)S(1)}, u32[]{:S(2)}, u32[]{:S(2)}) async-start(bf16[64,1,4,512]{3,2,1,0:T(4,128)(2,1)} %bitcast.10), calls=%async_computation.1 | async-start | bytes 524288 | tf_op jit(solution)/shard_map/all_to_all | solution.py:101
  261.6 1.0 broadcast_multiply_fusion.1
  262.9 0.9 copy.65
  263.7 6.7 %copy.62 = bf16[4,8,64,512]{2,1,3,0:T(8,128)(2,1)} copy(bf16[4,8,64,512]{3,1,0,2:T(8,128)(2,1)} %all-gather.6.cloned.1.call-done) | data formatting | bytes 4194304 | tf_op jit(solution)/shard_map/all_gather | solution.py:71
  270.4 6.7 %reshape_reshape.7 = bf16[4,512,8,16,4]{1,4,3,2,0:T(4,128)(2,1)} reshape(bf16[4,8,64,512]{2,1,3,0:T(8,128)(2,1)} %copy.62) | data formatting | bytes 4194304 | tf_op jit(solution)/shard_map/reshape;reshape | solution.py:78
  277.2 0.9 constant_dynamic-slice_fusion
  278.1 0.4 fusion
  278.6 0.8 reshape.235
  279.4 0.7 fusion.1
  280.1 0.8 reshape.233
  280.9 21.8 %all-to-all-done.1 = bf16[64,1,4,512]{3,2,1,0:T(4,128)(2,1)S(1)} async-done(((bf16[64,1,4,512]{3,2,1,0:T(4,128)(2,1)}), bf16[64,1,4,512]{3,2,1,0:T(4,128)(2,1)S(1)}, u32[]{:S(2)}, u32[]{:S(2)}) %all-to-all-start.1) | async-done | bytes 262176 | tf_op jit(solution)/shard_map/all_to_all | solution.py:101
  302.9 0.7 reshape.231
  (34 shorter events, 1.7 us)
Async XLA Ops:
  7.2 96.0 %all-gather.4.cloned.1.call-start = ((), (), s32[]{:S(2)}) async-start(), calls=%async_computation.2 | async-start | bytes 2228224 | tf_op jit(solution)/shard_map/all_gather | solution.py:72
  11.9 73.2 %copy-start.2 = (bf16[1,4,8,1,4,512]{5,4,3,2,1,0:T(4,128)(2,1)S(1)}, bf16[1,4,8,1,4,512]{5,4,3,2,1,0:T(4,128)(2,1)}, u32[]{:S(2)}) copy-start(bf16[1,4,8,1,4,512]{5,4,3,2,1,0:T(4,128)(2,1)} %param.11) | copy-start | bytes 393220
  11.9 73.4 %copy-start = (f32[1,4,8,1,4,512]{5,4,3,2,1,0:T(4,128)S(1)}, f32[1,4,8,1,4,512]{5,4,3,2,1,0:T(4,128)}, u32[]{:S(2)}) copy-start(f32[1,4,8,1,4,512]{5,4,3,2,1,0:T(4,128)} %param.13) | copy-start | bytes 786436
  11.9 71.8 %all-to-all-start = ((bf16[64,1,4,512]{3,2,1,0:T(4,128)(2,1)}), bf16[64,1,4,512]{3,2,1,0:T(4,128)(2,1)S(1)}, u32[]{:S(2)}, u32[]{:S(2)}) async-start(bf16[64,1,4,512]{3,2,1,0:T(4,128)(2,1)} %copy.55), calls=%async_computation | async-start | bytes 524288 | tf_op jit(solution)/shard_map/all_to_all | solution.py:54
  42.4 146.0 %all-gather.6.cloned.1.call-start = ((), (), s32[]{:S(2)}) async-start(), calls=%async_computation.3 | async-start | bytes 2228224 | tf_op jit(solution)/shard_map/all_gather | solution.py:71
  191.2 70.2 %copy-start.1 = (f32[1,4,8,1,4,512]{5,4,3,2,1,0:T(4,128)S(1)}, f32[1,4,8,1,4,512]{5,4,3,2,1,0:T(4,128)}, u32[]{:S(2)}) copy-start(f32[1,4,8,1,4,512]{5,4,3,2,1,0:T(4,128)} %param.10) | copy-start | bytes 786436
  229.7 73.0 %all-to-all-start.1 = ((bf16[64,1,4,512]{3,2,1,0:T(4,128)(2,1)}), bf16[64,1,4,512]{3,2,1,0:T(4,128)(2,1)S(1)}, u32[]{:S(2)}, u32[]{:S(2)}) async-start(bf16[64,1,4,512]{3,2,1,0:T(4,128)(2,1)} %bitcast.10), calls=%async_computation.1 | async-start | bytes 524288 | tf_op jit(solution)/shard_map/all_to_all | solution.py:101
Sparse Core Ops, SparseCore 0:
  12.2 90.9 all-gather.3
  107.9 80.4 all-gather.5
where the time goes:
time: 311 us; the launch traced here: 310 us
  waiting for transfers between devices  150 us (48%)
  starting transfers between devices  62.3 us (20%)
  local copies, waits for them, and re-layouts  44 us (14%)
  blocking collectives  31 us (10%)
  between operations  14.2 us (5%)
  matrix products  5.15 us (2%)
  other arithmetic  4.19 us (1%)
    all_gather x1, waiting for transfers between devices, body(): lax.all_gather(shaped, 'dp', axis=3, tiled=True)  81.3 us
    all_to_all x1, starting transfers between devices, body(): lax.all_to_all(returning, 'fsdp', split_axis=0, concat_axis=0, tiled=True)  31.7 us
    psum x1, blocking collectives, body(): adam_total, precond_total = lax.psum((adam_sq, precond_sq), 'dp')  31 us
    all_to_all x1, starting transfers between devices, body(): lax.all_to_all(outgoing, 'fsdp', split_axis=0, concat_axis=0, tiled=True)  30.5 us
    all_to_all x1, waiting for transfers between devices, body(): lax.all_to_all(outgoing, 'fsdp', split_axis=0, concat_axis=0, tiled=True)  28.1 us
    all_to_all x1, waiting for transfers between devices, body(): lax.all_to_all(returning, 'fsdp', split_axis=0, concat_axis=0, tiled=True)  21.8 us
    all_gather x1, waiting for transfers between devices, body(): lax.all_gather(right_root, 'dp', axis=3, tiled=True)  17.7 us
    scatter x1, local copies, waits for them, and re-layouts, block_tables(): jnp.zeros((owners, slot_count), jnp.int32).at[block_owner, slot_rank]  11.3 us
  transfers between devices with their start and end apart: 4, of which 4 were waited for; matrix products, arithmetic and copies ran while one was open for 14% of the time, Pallas kernels for 0%

commit v1 on v0

v1 whole, which is shorter than its diff:
```python
import functools
import jax
import jax.numpy as jnp
from jax import lax
from jax.experimental import pallas as pl
from jax.experimental.pallas import tpu as pltpu
from jax.sharding import PartitionSpec as P

FACTOR_DECAY = 0.999
MOMENT_DECAY = 0.95
ADAM_EPS = 1e-08
NORM_EPS = 1e-06
VMEM_LIMIT = 32 * 1024 * 1024
NORM_ROWS = 8

SMEM = pl.BlockSpec(memory_space=pltpu.SMEM)
VMEM = pl.BlockSpec(memory_space=pltpu.VMEM)


def call(kernel, out_shape, in_specs, out_specs, scratch_shapes=()):
    return pl.pallas_call(
        kernel,
        out_shape=out_shape,
        in_specs=in_specs,
        out_specs=out_specs,
        scratch_shapes=scratch_shapes,
        compiler_params=pltpu.CompilerParams(vmem_limit_bytes=VMEM_LIMIT),
    )


def dot(a, b, contract=(1, 0)):
    return lax.dot_general(
        a, b, (((contract[0],), (contract[1],)), ((), ())), preferred_element_type=jnp.float32
    )


def send_rows_kernel(shards, owner_ref, grad_ref, out_ref):
    width = out_ref.shape[2]
    count = grad_ref.shape[1] // width
    band = lax.axis_index("fsdp") // shards
    for column in range(count):
        owner = owner_ref[band * count + column]
        out_ref[owner] = grad_ref[:, column * width : (column + 1) * width]


def own_rows_kernel(
    band_ref, arrived_ref, moment_ref, left_ref, right_ref, out_ref, moment_out_ref, rows_ref
):
    slots, shards, dev_rows, width = moment_ref.shape
    rows = shards * dev_rows
    copies = out_ref.shape[0] // slots
    for slot in range(slots):
        band = band_ref[slot]
        total = jnp.zeros((dev_rows, width), jnp.float32)
        for shard in range(shards):
            values = arrived_ref[band * shards + shard].astype(jnp.float32)
            moment = (
                MOMENT_DECAY * moment_ref[slot, shard] + (1.0 - MOMENT_DECAY) * values * values
            )
            moment_out_ref[slot, shard] = moment
            adam = values / (jnp.sqrt(moment) + ADAM_EPS)
            total += adam * adam
            rows_ref[shard * dev_rows : (shard + 1) * dev_rows, :] = values
        own = rows_ref[...].astype(jnp.bfloat16)
        whole = jnp.sum(total, axis=(0, 1), keepdims=True)
        high = whole.astype(jnp.bfloat16).astype(jnp.float32)
        lane = lax.broadcasted_iota(jnp.int32, (NORM_ROWS, width), 1)
        norm = jnp.where(lane < width // 2, high, whole - high).astype(jnp.bfloat16)
        for copy in range(copies):
            place = copy * slots + slot
            out_ref[place, :rows, :] = own
            out_ref[place, rows : 2 * rows, :] = left_ref[slot]
            out_ref[place, 2 * rows : 3 * rows, :] = right_ref[slot]
            out_ref[place, 3 * rows :, :] = norm


def block_kernel(rows, slots, arrived_ref, order_ref, out_ref, grad_ref, precond_ref):
    width = order_ref.shape[0]
    span = slots * rows
    first = pl.multiple_of(lax.axis_index("dp") // slots * span, span)
    order = order_ref[...]
    grad = arrived_ref[:, :rows, :].reshape(width, width)
    left_root = arrived_ref[:, rows : 2 * rows, :].reshape(width, width)
    right_root = arrived_ref[:, 2 * rows : 3 * rows, :].reshape(width, width)
    by_device = dot(grad, order).astype(jnp.bfloat16)
    grad_ref[...] = by_device
    mixed = dot(left_root, by_device).astype(jnp.bfloat16)
    precond = dot(mixed, right_root)
    precond_ref[...] = precond
    norms = jnp.sum(arrived_ref[:, 3 * rows :, :].astype(jnp.float32), axis=0)
    half = width // 2
    adam_total = norms[:1, :1] + norms[:1, half : half + 1]
    precond_total = jnp.sum(precond * precond, axis=(0, 1), keepdims=True)
    scale = jnp.sqrt(adam_total) / jnp.sqrt(precond_total + NORM_EPS)
    update = (precond_ref[pl.ds(first, span), :] * scale).astype(jnp.bfloat16)
    left_gram = dot(grad_ref[pl.ds(first, span), :], by_device, (1, 1)).astype(jnp.bfloat16)
    left_gram = dot(left_gram, order, (1, 1)).astype(jnp.bfloat16)
    right_gram = dot(grad_ref[:, pl.ds(first, span)], grad, (0, 0)).astype(jnp.bfloat16)
    for place in range(slots):
        part = slice(place * rows, (place + 1) * rows)
        out_ref[place, :rows, :] = update[part]
        out_ref[place, rows : 2 * rows, :] = left_gram[part]
        out_ref[place, 2 * rows :, :] = right_gram[part]


def return_rows_kernel(shards, dev_rows, band_ref, back_ref, out_ref):
    for slot in range(back_ref.shape[0]):
        band = band_ref[slot]
        for shard in range(shards):
            out_ref[band * shards + shard] = back_ref[
                slot, shard * dev_rows : (shard + 1) * dev_rows, :
            ]


def place_rows_kernel(shards, owner_ref, returned_ref, out_ref):
    width = returned_ref.shape[2]
    count = out_ref.shape[1] // width
    band = lax.axis_index("fsdp") // shards
    for column in range(count):
        owner = owner_ref[band * count + column]
        out_ref[:, column * width : (column + 1) * width] = returned_ref[owner]


def owned_bands(block_owner, owner, slots, columns):
    ids = jnp.arange(block_owner.shape[0], dtype=jnp.int32)
    mine = block_owner == owner
    rank = jnp.sum((mine[None, :] & (ids[None, :] < ids[:, None])).astype(jnp.int32), axis=1)
    slot = jnp.arange(slots, dtype=jnp.int32)
    held = mine[None, :] & (rank[None, :] == slot[:, None])
    return jnp.sum(jnp.where(held, ids[None, :] // columns, 0), axis=1)


def device_order(shards, replicas, dev_rows):
    width = shards * replicas * dev_rows
    place = jnp.arange(width, dtype=jnp.int32)
    device, rest = place // (shards * dev_rows), place % (shards * dev_rows)
    row = (rest // dev_rows * replicas + device) * dev_rows + rest % dev_rows
    return (place[:, None] == row[None, :]).astype(jnp.bfloat16)


def body(grad, block_owner, left, right, left_root, right_root, moment):
    replicas = lax.axis_size("dp")
    owners = lax.axis_size("fsdp")
    dev_rows, columns_all = grad.shape[2:]
    _, slots, shards, _, _, width = left.shape
    rows = shards * dev_rows
    columns = columns_all // width
    groups = [list(range(i, i + slots)) for i in range(0, replicas, slots)]
    pieces = (owners, dev_rows, width)
    by_piece = (slots, shards, dev_rows, width)

    outgoing = call(
        functools.partial(send_rows_kernel, shards),
        jax.ShapeDtypeStruct(pieces, jnp.bfloat16),
        [SMEM, VMEM],
        VMEM,
    )(block_owner, grad.reshape(dev_rows, columns_all))
    arrived = lax.all_to_all(outgoing, "fsdp", split_axis=0, concat_axis=0, tiled=True)

    bands = owned_bands(block_owner, lax.axis_index("fsdp"), slots, columns)
    order = device_order(shards, replicas, dev_rows)
    left_rows = dot(left_root.reshape(slots * rows, width), order).astype(jnp.bfloat16)
    packed, moment_new = call(
        own_rows_kernel,
        (
            jax.ShapeDtypeStruct((replicas, 3 * rows + NORM_ROWS, width), jnp.bfloat16),
            jax.ShapeDtypeStruct(by_piece, jnp.float32),
        ),
        [SMEM, VMEM, VMEM, VMEM, VMEM],
        (VMEM, VMEM),
        [pltpu.VMEM((rows, width), jnp.float32)],
    )(
        bands,
        arrived,
        moment.reshape(by_piece),
        left_rows.reshape(slots, rows, width),
        right_root.reshape(slots, rows, width),
    )
    gathered = lax.all_to_all(packed, "dp", split_axis=0, concat_axis=0, tiled=True)

    results = call(
        functools.partial(block_kernel, rows, slots),
        jax.ShapeDtypeStruct((slots, 3 * rows, width), jnp.bfloat16),
        [VMEM, VMEM],
        VMEM,
        [pltpu.VMEM((width, width), jnp.bfloat16), pltpu.VMEM((width, width), jnp.float32)],
    )(gathered, order)
    back = lax.all_to_all(
        results, "dp", split_axis=0, concat_axis=0, tiled=True, axis_index_groups=groups
    )

    returning = call(
        functools.partial(return_rows_kernel, shards, dev_rows),
        jax.ShapeDtypeStruct(pieces, jnp.bfloat16),
        [SMEM, VMEM],
        VMEM,
    )(bands, back)
    returned = lax.all_to_all(returning, "fsdp", split_axis=0, concat_axis=0, tiled=True)
    update = call(
        functools.partial(place_rows_kernel, shards),
        jax.ShapeDtypeStruct((dev_rows, columns_all), jnp.bfloat16),
        [SMEM, VMEM],
        VMEM,
    )(block_owner, returned)

    def factor(old, gram):
        gram = gram.astype(jnp.float32).reshape(old.shape)
        return FACTOR_DECAY * old + (1.0 - FACTOR_DECAY) * gram

    return (
        update.reshape(grad.shape),
        factor(left, back[:, rows : 2 * rows]),
        factor(right, back[:, 2 * rows :]),
        moment_new.reshape(moment.shape),
    )


def solution(mesh):
    state = P("fsdp", None, None, "dp", None, None)
    rows = P("fsdp", "dp", None, None)
    return jax.shard_map(
        body,
        mesh=mesh,
        in_specs=(rows, P(), state, state, state, state, state),
        out_specs=(rows, state, state, state),
        check_vma=False,
    )
```

time: 311 us -> 171 us (0.55)
  waiting for transfers between devices: 150 us -> 99.5 us
  local copies, waits for them, and re-layouts: 44 us -> 3.67 us
  blocking collectives: 31 us -> 8.62 us
  starting transfers between devices: 62.3 us -> 48.2 us
  between operations: 14.2 us -> 0.76 us
  Pallas kernels: 0 us -> 7.42 us
  matrix products: 5.15 us -> 0.33 us
    all_gather x2 -> x0, waiting for transfers between devices: 99 us -> none  [the longest x1 81.3 us: body(): lax.all_gather(shaped, 'dp', axis=3, tiled=True)]
    psum x1 -> x0, blocking collectives: 31 us -> none  [body(): adam_total, precond_total = lax.psum((adam_sq, precond_sq), 'dp')]
    all_to_all x0 -> x1, waiting for transfers between devices: none -> 21.3 us  [body(): lax.all_to_all(packed, 'dp', split_axis=0, concat_axis=0, tiled=True)]
    all_to_all x1, starting transfers between devices: 31.7 us -> 11.1 us  [body(): lax.all_to_all(returning, 'fsdp', split_axis=0, concat_axis=0, tiled=True)]
    all_to_all x1, waiting for transfers between devices: 21.8 us -> 40.1 us  [body(): lax.all_to_all(returning, 'fsdp', split_axis=0, concat_axis=0, tiled=True)]
    scatter x2 -> x0, local copies, waits for them, and re-layouts: 15.3 us -> none  [the longest x1 11.3 us: block_tables(): jnp.zeros((owners, slot_count), jnp.int32).at[block_owner, slot_rank]]
    all_to_all x1, waiting for transfers between devices: 28.1 us -> 38.1 us  [body(): lax.all_to_all(outgoing, 'fsdp', split_axis=0, concat_axis=0, tiled=True)]
    all_gather x2 -> x0, local copies, waits for them, and re-layouts: 9.43 us -> none  [body(): lax.all_gather(shaped, 'dp', axis=3, tiled=True)]
  transfers between devices with their start and end apart: 4 -> 3, of which waited for: 4 -> 3; matrix products, arithmetic and copies ran while one was open for 14% -> 3% of each run, Pallas kernels for 0% -> 0%
where the time goes in v1:
time: 171 us
  waiting for transfers between devices  99.5 us (58%)
  starting transfers between devices  48.2 us (28%)
  blocking collectives  8.62 us (5%)
  Pallas kernels  7.42 us (4%)
  local copies, waits for them, and re-layouts  3.67 us (2%)
  other arithmetic  2.1 us (1%)
    all_to_all x1, waiting for transfers between devices, body(): lax.all_to_all(returning, 'fsdp', split_axis=0, concat_axis=0, tiled=True)  40.1 us
    all_to_all x1, waiting for transfers between devices, body(): lax.all_to_all(outgoing, 'fsdp', split_axis=0, concat_axis=0, tiled=True)  38.1 us
    all_to_all x1, starting transfers between devices, body(): lax.all_to_all(outgoing, 'fsdp', split_axis=0, concat_axis=0, tiled=True)  30.4 us
    all_to_all x1, waiting for transfers between devices, body(): lax.all_to_all(packed, 'dp', split_axis=0, concat_axis=0, tiled=True)  21.3 us
    all_to_all x1, starting transfers between devices, body(): lax.all_to_all(returning, 'fsdp', split_axis=0, concat_axis=0, tiled=True)  11.1 us
    all_to_all x1, blocking collectives, body(): lax.all_to_all(results, 'dp', split_axis=0, concat_axis=0, tiled=True, ax...  8.62 us
    all_to_all x1, starting transfers between devices, body(): lax.all_to_all(packed, 'dp', split_axis=0, concat_axis=0, tiled=True)  6.76 us
  transfers between devices with their start and end apart: 3, of which 3 were waited for; matrix products, arithmetic and copies ran while one was open for 3% of the time, Pallas kernels for 0%

profile of v1, /device:TPU:1, one launch (start us, length us, event | category | flops | bytes accessed | tf_op | source)
XLA Modules:
  0.0 170.6 jit_solution(14767590264459682160)
XLA Ops:
  0.6 0.0 copy-start
  0.6 0.0 copy-start.1
  0.7 0.9 copy-done.1
  1.6 0.7 copy-done.2
  2.3 1.3 shard_map.102
  3.6 30.4 %all-to-all-start = ((bf16[64,4,512]{2,1,0:T(4,128)(2,1)}), bf16[64,4,512]{2,1,0:T(4,128)(2,1)S(1)}, u32[]{:S(2)}, u32[]{:S(2)}) async-start(bf16[64,4,512]{2,1,0:T(4,128)(2,1)} %shard_map.102), calls=%async_computation | async-start | bytes 524288 | tf_op jit(solution)/shard_map/all_to_all | solution.py:158
  34.0 0.9 reshape.150
  34.9 0.9 reshape.152.right_ref
  35.9 0.7 broadcast_compare_fusion
  36.6 0.1 convert_reduce_fusion
  36.7 0.1 select_reduce_fusion.band_ref
  36.8 0.3 convolution_convert_fusion
  37.2 38.1 %all-to-all-done.arrived_ref = bf16[64,4,512]{2,1,0:T(4,128)(2,1)S(1)} async-done(((bf16[64,4,512]{2,1,0:T(4,128)(2,1)}), bf16[64,4,512]{2,1,0:T(4,128)(2,1)S(1)}, u32[]{:S(2)}, u32[]{:S(2)}) %all-to-all-start) | async-done | bytes 262176 | tf_op jit(solution)/shard_map/all_to_all | solution.py:158
  75.3 0.0 copy-done
  75.3 2.1 %shard_map.103 = (bf16[16,104,512]{2,1,0:T(8,128)(2,1)}, f32[4,8,4,512]{3,2,1,0:T(4,128)}) custom-call(s32[4]{0:T(128)S(1)} %select_reduce_fusion.band_ref, bf16[64,4,512]{2,1,0:T(4,128)(2,1)S(1)} %all-to-all-done.arrived_ref, f32[4,8,4,512]{3,2,1,0:T(4,128)S(1)} %bitcast.14, bf16[4,32,512]{2,1,0:T(8,128)(2,1)S(1)} %bitcast.16, ...), custom_call_target="tpu_custom_call" | custom-call | tf_op jit(solution)/shard_map/pallas_call | solution.py:163
  77.4 6.8 %all-to-all-start.1 = ((bf16[16,104,512]{2,1,0:T(8,128)(2,1)}), bf16[16,104,512]{2,1,0:T(8,128)(2,1)S(1)}, u32[]{:S(2)}, u32[]{:S(2)}) async-start(bf16[16,104,512]{2,1,0:T(8,128)(2,1)} %get-tuple-element.6), calls=%async_computation.1 | async-start | bytes 3407872 | tf_op jit(solution)/shard_map/all_to_all | solution.py:179
  84.1 0.1 fusion.order_ref
  84.3 21.3 %all-to-all-done.1.arrived_ref = bf16[16,104,512]{2,1,0:T(8,128)(2,1)S(1)} async-done(((bf16[16,104,512]{2,1,0:T(8,128)(2,1)}), bf16[16,104,512]{2,1,0:T(8,128)(2,1)S(1)}, u32[]{:S(2)}, u32[]{:S(2)}) %all-to-all-start.1) | async-done | bytes 1703968 | tf_op jit(solution)/shard_map/all_to_all | solution.py:179
  105.6 1.5 shard_map.104
  107.1 8.6 %all_to_all.20.back_ref = bf16[4,96,512]{2,1,0:T(8,128)(2,1)S(1)} all-to-all(bf16[4,96,512]{2,1,0:T(8,128)(2,1)S(1)} %shard_map.104), channel_id=1, replica_groups={{0,64,128,192},{256,320,384,448},{512,576,640,704},{768,832,896,960},{1..., dimensions={0} | all-to-all | bytes 786432 | tf_op jit(solution)/shard_map/all_to_all | solution.py:188
  115.7 1.3 shard_map.105
  117.0 11.1 %all-to-all-start.3 = ((bf16[64,4,512]{2,1,0:T(4,128)(2,1)}), bf16[64,4,512]{2,1,0:T(4,128)(2,1)S(1)}, u32[]{:S(2)}, u32[]{:S(2)}) async-start(bf16[64,4,512]{2,1,0:T(4,128)(2,1)} %shard_map.105), calls=%async_computation.3 | async-start | bytes 524288 | tf_op jit(solution)/shard_map/all_to_all | solution.py:198
  128.0 0.0 copy-start.3
  128.1 0.1 convert_multiply_fusion
  128.1 0.1 mul.61
  128.2 0.1 mul.64
  128.3 0.0 copy-done.4
  128.3 0.0 copy-done.5
  128.3 1.0 bitcast_add_fusion
  129.3 40.1 %all-to-all-done.3.returned_ref = bf16[64,4,512]{2,1,0:T(4,128)(2,1)S(1)} async-done(((bf16[64,4,512]{2,1,0:T(4,128)(2,1)}), bf16[64,4,512]{2,1,0:T(4,128)(2,1)S(1)}, u32[]{:S(2)}, u32[]{:S(2)}) %all-to-all-start.3) | async-done | bytes 262176 | tf_op jit(solution)/shard_map/all_to_all | solution.py:198
  169.3 0.0 copy-done.3
  169.3 1.3 shard_map.106
  (5 shorter events, 0.0 us)
Async XLA Ops:
  0.6 74.6 %copy-start = (f32[1,4,8,1,4,512]{5,4,3,2,1,0:T(4,128)S(1)}, f32[1,4,8,1,4,512]{5,4,3,2,1,0:T(4,128)}, u32[]{:S(2)}) copy-start(f32[1,4,8,1,4,512]{5,4,3,2,1,0:T(4,128)} %param.13) | copy-start | bytes 786436
  0.6 0.9 copy-start.1
  1.6 0.7 copy-start.2
  3.6 71.7 %all-to-all-start = ((bf16[64,4,512]{2,1,0:T(4,128)(2,1)}), bf16[64,4,512]{2,1,0:T(4,128)(2,1)S(1)}, u32[]{:S(2)}, u32[]{:S(2)}) async-start(bf16[64,4,512]{2,1,0:T(4,128)(2,1)} %shard_map.102), calls=%async_computation | async-start | bytes 524288 | tf_op jit(solution)/shard_map/all_to_all | solution.py:158
  77.4 28.2 %all-to-all-start.1 = ((bf16[16,104,512]{2,1,0:T(8,128)(2,1)}), bf16[16,104,512]{2,1,0:T(8,128)(2,1)S(1)}, u32[]{:S(2)}, u32[]{:S(2)}) async-start(bf16[16,104,512]{2,1,0:T(8,128)(2,1)} %get-tuple-element.6), calls=%async_computation.1 | async-start | bytes 3407872 | tf_op jit(solution)/shard_map/all_to_all | solution.py:179
  115.7 12.6 %copy-start.4 = (f32[1,4,8,1,4,512]{5,4,3,2,1,0:T(4,128)S(1)}, f32[1,4,8,1,4,512]{5,4,3,2,1,0:T(4,128)}, u32[]{:S(2)}) copy-start(f32[1,4,8,1,4,512]{5,4,3,2,1,0:T(4,128)} %param.10) | copy-start | bytes 786436
  115.7 12.6 %copy-start.5 = (f32[1,4,8,1,4,512]{5,4,3,2,1,0:T(4,128)S(1)}, f32[1,4,8,1,4,512]{5,4,3,2,1,0:T(4,128)}, u32[]{:S(2)}) copy-start(f32[1,4,8,1,4,512]{5,4,3,2,1,0:T(4,128)} %param.9) | copy-start | bytes 786436
  117.0 52.4 %all-to-all-start.3 = ((bf16[64,4,512]{2,1,0:T(4,128)(2,1)}), bf16[64,4,512]{2,1,0:T(4,128)(2,1)S(1)}, u32[]{:S(2)}, u32[]{:S(2)}) async-start(bf16[64,4,512]{2,1,0:T(4,128)(2,1)} %shard_map.105), calls=%async_computation.3 | async-start | bytes 524288 | tf_op jit(solution)/shard_map/all_to_all | solution.py:198
  128.0 41.3 %copy-start.3 = (s32[256]{0:T(256)S(1)}, s32[256]{0:T(256)}, u32[]{:S(2)}) copy-start(s32[256]{0:T(256)} %owner_ref.3) | copy-start | bytes 3076

commit v2 on v1

--- a/solution.py
+++ b/solution.py
@@ -15,6 +15,23 @@
 
 SMEM = pl.BlockSpec(memory_space=pltpu.SMEM)
 VMEM = pl.BlockSpec(memory_space=pltpu.VMEM)
+ANY = pl.BlockSpec(memory_space=pl.ANY)
+
+
+ORDER_STEP = 31
+ORDER_FIRST = 22
+
+
+def place_of(owner, owners):
+    half = owners // 2
+    back = pow(ORDER_STEP, -1, half)
+    return lax.rem(owner, 2) * half + lax.rem((owner // 2 + half - ORDER_FIRST) * back, half)
+
+
+def exchange_order(owners):
+    half = owners // 2
+    chips = [(ORDER_FIRST + i * ORDER_STEP) % half for i in range(half)]
+    return [[2 * chip + core for core in range(2) for chip in chips]]
 
 
 def call(kernel, out_shape, in_specs, out_specs, scratch_shapes=()):
@@ -40,20 +57,20 @@
     band = lax.axis_index("fsdp") // shards
     for column in range(count):
         owner = owner_ref[band * count + column]
-        out_ref[owner] = grad_ref[:, column * width : (column + 1) * width]
-
-
-def own_rows_kernel(
-    band_ref, arrived_ref, moment_ref, left_ref, right_ref, out_ref, moment_out_ref, rows_ref
-):
+        out_ref[place_of(owner, out_ref.shape[0])] = grad_ref[:, column * width : (column + 1) * width]
+
+
+def own_rows_kernel(band_ref, arrived_ref, moment_ref, *refs):
+    out_ref, moment_out_ref, rows_ref = refs[-3:]
     slots, shards, dev_rows, width = moment_ref.shape
+    owners = arrived_ref.shape[0]
     rows = shards * dev_rows
     copies = out_ref.shape[0] // slots
     for slot in range(slots):
         band = band_ref[slot]
         total = jnp.zeros((dev_rows, width), jnp.float32)
         for shard in range(shards):
-            values = arrived_ref[band * shards + shard].astype(jnp.float32)
+            values = arrived_ref[place_of(band * shards + shard, owners)].astype(jnp.float32)
             moment = (
                 MOMENT_DECAY * moment_ref[slot, shard] + (1.0 - MOMENT_DECAY) * values * values
             )
@@ -69,45 +86,80 @@
         for copy in range(copies):
             place = copy * slots + slot
             out_ref[place, :rows, :] = own
-            out_ref[place, rows : 2 * rows, :] = left_ref[slot]
-            out_ref[place, 2 * rows : 3 * rows, :] = right_ref[slot]
-            out_ref[place, 3 * rows :, :] = norm
-
-
-def block_kernel(rows, slots, arrived_ref, order_ref, out_ref, grad_ref, precond_ref):
+            out_ref[place, rows:, :] = norm
+
+
+def split_roots_kernel(left_ref, right_ref, order_ref, *refs):
+    out_refs, rows_ref = refs[:-1], refs[-1]
+    slots, rows, width = right_ref.shape
+    place = lax.rem(lax.axis_index("dp"), slots)
+    left = dot(left_ref[...].reshape(slots * rows, width), order_ref[...])
+    rows_ref[...] = left.astype(jnp.bfloat16).reshape(slots, rows, width)
+    for step, out_ref in enumerate(out_refs):
+        slot = lax.rem(place + step, slots)
+        out_ref[:rows, :] = rows_ref[slot]
+        out_ref[rows:, :] = right_ref[slot]
+
+
+def block_kernel(rows, slots, arrived_ref, order_ref, *refs):
+    *root_refs, out_ref, precond_ref, left_ref, right_ref = refs
     width = order_ref.shape[0]
     span = slots * rows
-    first = pl.multiple_of(lax.axis_index("dp") // slots * span, span)
+    device = lax.axis_index("dp")
+    first = pl.multiple_of(device // slots * span, span)
+    lines = len(root_refs)
+    for step, root_ref in enumerate(root_refs):
+        line = lax.rem(device // slots + lines - step, lines)
+        for part in range(slots):
+            source = line * slots + lax.rem(device + slots - part, slots)
+            place = pl.ds(pl.multiple_of(source * rows, rows), rows)
+            left_ref[place, :] = root_ref[2 * part * rows : (2 * part + 1) * rows, :]
+            right_ref[place, :] = root_ref[(2 * part + 1) * rows : (2 * part + 2) * rows, :]
     order = order_ref[...]
     grad = arrived_ref[:, :rows, :].reshape(width, width)
-    left_root = arrived_ref[:, rows : 2 * rows, :].reshape(width, width)
-    right_root = arrived_ref[:, 2 * rows : 3 * rows, :].reshape(width, width)
     by_device = dot(grad, order).astype(jnp.bfloat16)
-    grad_ref[...] = by_device
-    mixed = dot(left_root, by_device).astype(jnp.bfloat16)
-    precond = dot(mixed, right_root)
+    mixed = dot(left_ref[...], by_device).astype(jnp.bfloat16)
+    precond = dot(mixed, right_ref[...])
     precond_ref[...] = precond
-    norms = jnp.sum(arrived_ref[:, 3 * rows :, :].astype(jnp.float32), axis=0)
+    norms = jnp.sum(arrived_ref[:, rows:, :].astype(jnp.float32), axis=0)
     half = width // 2
     adam_total = norms[:1, :1] + norms[:1, half : half + 1]
     precond_total = jnp.sum(precond * precond, axis=(0, 1), keepdims=True)
     scale = jnp.sqrt(adam_total) / jnp.sqrt(precond_total + NORM_EPS)
     update = (precond_ref[pl.ds(first, span), :] * scale).astype(jnp.bfloat16)
+    for place in range(slots):
+        out_ref[place] = update[place * rows : (place + 1) * rows]
+
+
+def gram_kernel(rows, arrived_ref, order_ref, _, *refs):
+    out_refs, grad_ref = refs[:-1], refs[-1]
+    slots = len(out_refs)
+    width = order_ref.shape[0]
+    device = lax.axis_index("dp")
+    order = order_ref[...]
+    grad = arrived_ref[:, :rows, :].reshape(width, width)
+    by_device = dot(grad, order).astype(jnp.bfloat16)
+    grad_ref[...] = by_device
+    span = slots * rows
+    first = pl.multiple_of(device // slots * span, span)
     left_gram = dot(grad_ref[pl.ds(first, span), :], by_device, (1, 1)).astype(jnp.bfloat16)
     left_gram = dot(left_gram, order, (1, 1)).astype(jnp.bfloat16)
     right_gram = dot(grad_ref[:, pl.ds(first, span)], grad, (0, 0)).astype(jnp.bfloat16)
-    for place in range(slots):
-        part = slice(place * rows, (place + 1) * rows)
-        out_ref[place, :rows, :] = update[part]
-        out_ref[place, rows : 2 * rows, :] = left_gram[part]
-        out_ref[place, 2 * rows :, :] = right_gram[part]
+    for step, out_ref in enumerate(out_refs):
+        for place in range(slots):
+
+            @pl.when(lax.rem(device + step, slots) == place)
+            def _():
+                part = slice(place * rows, (place + 1) * rows)
+                out_ref[:rows, :] = left_gram[part]
+                out_ref[rows:, :] = right_gram[part]
 
 
 def return_rows_kernel(shards, dev_rows, band_ref, back_ref, out_ref):
     for slot in range(back_ref.shape[0]):
         band = band_ref[slot]
         for shard in range(shards):
-            out_ref[band * shards + shard] = back_ref[
+            out_ref[place_of(band * shards + shard, out_ref.shape[0])] = back_ref[
                 slot, shard * dev_rows : (shard + 1) * dev_rows, :
             ]
 
@@ -118,7 +170,25 @@
     band = lax.axis_index("fsdp") // shards
     for column in range(count):
         owner = owner_ref[band * count + column]
-        out_ref[:, column * width : (column + 1) * width] = returned_ref[owner]
+        out_ref[:, column * width : (column + 1) * width] = returned_ref[
+            place_of(owner, returned_ref.shape[0])
+        ]
+
+
+def factors_kernel(left_ref, right_ref, *refs):
+    gram_refs, out_refs = refs[:-2], refs[-2:]
+    slots, shards, dev_rows, _ = left_ref.shape
+    rows = shards * dev_rows
+    place = lax.rem(lax.axis_index("dp"), slots)
+    for step, gram_ref in enumerate(gram_refs):
+        slot = lax.rem(place + slots - step, slots)
+        for side, (old_ref, out_ref) in enumerate(zip((left_ref, right_ref), out_refs)):
+            for shard in range(shards):
+                first = side * rows + shard * dev_rows
+                gram = gram_ref[first : first + dev_rows, :].astype(jnp.float32)
+                out_ref[slot, shard] = (
+                    FACTOR_DECAY * old_ref[slot, shard] + (1.0 - FACTOR_DECAY) * gram
+                )
 
 
 def owned_bands(block_owner, owner, slots, columns):
@@ -146,6 +216,7 @@
     rows = shards * dev_rows
     columns = columns_all // width
     groups = [list(range(i, i + slots)) for i in range(0, replicas, slots)]
+    turns = exchange_order(owners)
     pieces = (owners, dev_rows, width)
     by_piece = (slots, shards, dev_rows, width)
 
@@ -155,36 +226,56 @@
         [SMEM, VMEM],
         VMEM,
     )(block_owner, grad.reshape(dev_rows, columns_all))
-    arrived = lax.all_to_all(outgoing, "fsdp", split_axis=0, concat_axis=0, tiled=True)
+    arrived = lax.all_to_all(outgoing, "fsdp", split_axis=0, concat_axis=0, tiled=True, axis_index_groups=turns)
 
     bands = owned_bands(block_owner, lax.axis_index("fsdp"), slots, columns)
     order = device_order(shards, replicas, dev_rows)
-    left_rows = dot(left_root.reshape(slots * rows, width), order).astype(jnp.bfloat16)
+    both = jax.ShapeDtypeStruct((2 * rows, width), jnp.bfloat16)
+    own_part, *parts = call(
+        split_roots_kernel,
+        (both,) * slots,
+        [VMEM, VMEM, VMEM],
+        (VMEM,) * slots,
+        [pltpu.VMEM((slots, rows, width), jnp.bfloat16)],
+    )(left_root.reshape(slots, rows, width), right_root.reshape(slots, rows, width), order)
+    lines = replicas // slots
+    devices = [(line, place) for line in range(lines) for place in range(slots)]
+
+    def along_line(part, step):
+        pairs = [(i * slots + j, i * slots + (j + step) % slots) for i, j in devices]
+        return lax.ppermute(part, "dp", pairs)
+
+    parts = [along_line(part, step) for step, part in enumerate(parts, 1)]
+    line_roots = jnp.concatenate([own_part, *parts])
+    roots = [line_roots]
+    for step in range(1, lines):
+        pairs = [(i * slots + j, (i + step) % lines * slots + j) for i, j in devices]
+        roots.append(lax.ppermute(line_roots, "dp", pairs))
+
+    early = roots[:2] + roots[3:]
     packed, moment_new = call(
         own_rows_kernel,
         (
-            jax.ShapeDtypeStruct((replicas, 3 * rows + NORM_ROWS, width), jnp.bfloat16),
+            jax.ShapeDtypeStruct((replicas, rows + NORM_ROWS, width), jnp.bfloat16),
             jax.ShapeDtypeStruct(by_piece, jnp.float32),
         ),
-        [SMEM, VMEM, VMEM, VMEM, VMEM],
+        [SMEM, VMEM, VMEM] + [ANY] * len(early),
         (VMEM, VMEM),
         [pltpu.VMEM((rows, width), jnp.float32)],
-    )(
-        bands,
-        arrived,
-        moment.reshape(by_piece),
-        left_rows.reshape(slots, rows, width),
-        right_root.reshape(slots, rows, width),
-    )
+    )(bands, arrived, moment.reshape(by_piece), *early)
     gathered = lax.all_to_all(packed, "dp", split_axis=0, concat_axis=0, tiled=True)
 
     results = call(
         functools.partial(block_kernel, rows, slots),
-        jax.ShapeDtypeStruct((slots, 3 * rows, width), jnp.bfloat16),
-        [VMEM, VMEM],
+        jax.ShapeDtypeStruct((slots, rows, width), jnp.bfloat16),
+        [VMEM] * (2 + lines),
         VMEM,
-        [pltpu.VMEM((width, width), jnp.bfloat16), pltpu.VMEM((width, width), jnp.float32)],
-    )(gathered, order)
+        [
+            pltpu.VMEM((width, width), jnp.float32),
+            pltpu.VMEM((width, width), jnp.bfloat16),
+            pltpu.VMEM((width, width), jnp.bfloat16),
+        ],
+    )(gathered, order, *roots)
     back = lax.all_to_all(
         results, "dp", split_axis=0, concat_axis=0, tiled=True, axis_index_groups=groups
     )
@@ -195,22 +286,33 @@
         [SMEM, VMEM],
         VMEM,
     )(bands, back)
-    returned = lax.all_to_all(returning, "fsdp", split_axis=0, concat_axis=0, tiled=True)
+    returned = lax.all_to_all(returning, "fsdp", split_axis=0, concat_axis=0, tiled=True, axis_index_groups=turns)
+
+    own_grams, *grams = call(
+        functools.partial(gram_kernel, rows),
+        (both,) * slots,
+        [VMEM, VMEM, ANY],
+        (VMEM,) * slots,
+        [pltpu.VMEM((width, width), jnp.bfloat16)],
+    )(gathered, order, returning)
+    grams = [own_grams, *(along_line(part, step) for step, part in enumerate(grams, 1))]
+    left_new, right_new = call(
+        factors_kernel,
+        (jax.ShapeDtypeStruct(by_piece, jnp.float32),) * 2,
+        [VMEM] * (2 + slots),
+        (VMEM, VMEM),
+    )(left.reshape(by_piece), right.reshape(by_piece), *grams)
+
     update = call(
         functools.partial(place_rows_kernel, shards),
         jax.ShapeDtypeStruct((dev_rows, columns_all), jnp.bfloat16),
         [SMEM, VMEM],
         VMEM,
     )(block_owner, returned)
-
-    def factor(old, gram):
-        gram = gram.astype(jnp.float32).reshape(old.shape)
-        return FACTOR_DECAY * old + (1.0 - FACTOR_DECAY) * gram
-
     return (
         update.reshape(grad.shape),
-        factor(left, back[:, rows : 2 * rows]),
-        factor(right, back[:, 2 * rows :]),
+        left_new.reshape(left.shape),
+        right_new.reshape(right.shape),
         moment_new.reshape(moment.shape),
     )
 

time: 171 us -> 152 us (0.89)
  waiting for transfers between devices: 99.5 us -> 41 us
  starting transfers between devices: 48.2 us -> 88.2 us
  Pallas kernels: 7.42 us -> 9.88 us
  other arithmetic: 2.1 us -> 0.39 us
    all_to_all x2, waiting for transfers between devices: 78.2 us -> 20.6 us  [the longest x1 16.4 us: body(): lax.all_to_all(returning, 'fsdp', split_axis=0, concat_axis=0, tiled=True...]
    ppermute x0 -> x9, starting transfers between devices: none -> 30.4 us  [the longest x6 19.1 us: along_line(): return lax.ppermute(part, 'dp', pairs)]
    all_to_all x1, waiting for transfers between devices: 21.3 us -> 0.01 us  [body(): lax.all_to_all(packed, 'dp', split_axis=0, concat_axis=0, tiled=True)]
    ppermute x0 -> x9, waiting for transfers between devices: none -> 20.3 us  [the longest x3 15.3 us: body(): roots.append(lax.ppermute(line_roots, 'dp', pairs))]
    all_to_all x2, starting transfers between devices: 41.5 us -> 51.1 us  [the longest x1 31.2 us: body(): lax.all_to_all(outgoing, 'fsdp', split_axis=0, concat_axis=0, tiled=True,...]
    pallas_call x1 -> x4, Pallas kernels: 2.11 us -> 4.02 us  [the longest x1 1.8 us: body(): call(own_rows_kernel, (jax.ShapeDtypeStruct((replicas, rows + NORM_ROWS,...]
  transfers between devices with their start and end apart: 3 -> 12, of which waited for: 3 -> 8; matrix products, arithmetic and copies ran while one was open for 3% -> 0% of each run, Pallas kernels for 0% -> 1%
where the time goes in v2:
time: 152 us; the launch traced here: 151 us
  starting transfers between devices  88.2 us (58%)
  waiting for transfers between devices  41 us (27%)
  Pallas kernels  9.88 us (7%)
  blocking collectives  8.59 us (6%)
  local copies, waits for them, and re-layouts  2.56 us (2%)
    all_to_all x1, starting transfers between devices, body(): lax.all_to_all(outgoing, 'fsdp', split_axis=0, concat_axis=0, tiled=True,...  31.2 us
    all_to_all x1, starting transfers between devices, body(): lax.all_to_all(returning, 'fsdp', split_axis=0, concat_axis=0, tiled=True...  19.9 us
    ppermute x6, starting transfers between devices, along_line(): return lax.ppermute(part, 'dp', pairs)  19.1 us
    all_to_all x1, waiting for transfers between devices, body(): lax.all_to_all(returning, 'fsdp', split_axis=0, concat_axis=0, tiled=True...  16.4 us
    ppermute x3, waiting for transfers between devices, body(): roots.append(lax.ppermute(line_roots, 'dp', pairs))  15.3 us
    ppermute x3, starting transfers between devices, body(): roots.append(lax.ppermute(line_roots, 'dp', pairs))  11.3 us
    all_to_all x1, blocking collectives, body(): lax.all_to_all(results, 'dp', split_axis=0, concat_axis=0, tiled=True, ax...  8.59 us
    all_to_all x1, starting transfers between devices, body(): lax.all_to_all(packed, 'dp', split_axis=0, concat_axis=0, tiled=True)  6.76 us
  transfers between devices with their start and end apart: 12, of which 8 were waited for; matrix products, arithmetic and copies ran while one was open for 0% of the time, Pallas kernels for 1%

profile of v2, /device:TPU:1, one launch (start us, length us, event | category | flops | bytes accessed | tf_op | source)
XLA Modules:
  0.0 151.5 jit_solution(14383787339506356344)
XLA Ops:
  0.6 0.7 copy-done.4
  1.3 0.9 copy-done.3
  2.2 1.5 %shard_map.102 = bf16[64,4,512]{2,1,0:T(4,128)(2,1)} custom-call(s32[256]{0:T(256)S(1)} %copy-done.4, bf16[4,16384]{1,0:T(4,128)(2,1)S(1)} %bitcast.17), custom_call_target="tpu_custom_call" | custom-call | tf_op jit(solution)/shard_map/pallas_call | solution.py:223
  3.7 31.2 %all-to-all-start = ((bf16[64,4,512]{2,1,0:T(4,128)(2,1)}), bf16[64,4,512]{2,1,0:T(4,128)(2,1)S(1)}, u32[]{:S(2)}, u32[]{:S(2)}) async-start(bf16[64,4,512]{2,1,0:T(4,128)(2,1)} %shard_map.102), calls=%async_computation | async-start | bytes 524288 | tf_op jit(solution)/shard_map/all_to_all | solution.py:229
  35.0 0.9 copy-done.6
  36.0 0.2 shard_map.103
  36.3 3.2 %collective-permute-start = (bf16[64,512]{1,0:T(8,128)(2,1)S(1)}, bf16[64,512]{1,0:T(8,128)(2,1)S(1)}, u32[]{:S(2)}, u32[]{:S(2)}) collective-permute-start(bf16[64,512]{1,0:T(8,128)(2,1)S(1)} %get-tuple-element.17), channel_id=1, source_target_pairs={{0,64},{64,128},{128,192},{192,0},{256,320},{320,384},{384,448},{4... | collective-permute-start | bytes 196616 | tf_op jit(solution)/shard_map/ppermute | solution.py:246
  39.5 4.5 %collective-permute-start.1 = (bf16[64,512]{1,0:T(8,128)(2,1)S(1)}, bf16[64,512]{1,0:T(8,128)(2,1)S(1)}, u32[]{:S(2)}, u32[]{:S(2)}) collective-permute-start(bf16[64,512]{1,0:T(8,128)(2,1)S(1)} %get-tuple-element.18), channel_id=1, source_target_pairs={{0,128},{64,192},{128,0},{192,64},{256,384},{320,448},{384,256},{4... | collective-permute-start | bytes 196616 | tf_op jit(solution)/shard_map/ppermute | solution.py:246
  44.0 3.0 %collective-permute-start.2 = (bf16[64,512]{1,0:T(8,128)(2,1)S(1)}, bf16[64,512]{1,0:T(8,128)(2,1)S(1)}, u32[]{:S(2)}, u32[]{:S(2)}) collective-permute-start(bf16[64,512]{1,0:T(8,128)(2,1)S(1)} %get-tuple-element.19), channel_id=1, source_target_pairs={{0,192},{64,0},{128,64},{192,128},{256,448},{320,256},{384,320},{4... | collective-permute-start | bytes 196616 | tf_op jit(solution)/shard_map/ppermute | solution.py:246
  47.1 2.2 %collective-permute-done.2 = bf16[64,512]{1,0:T(8,128)(2,1)S(1)} collective-permute-done((bf16[64,512]{1,0:T(8,128)(2,1)S(1)}, bf16[64,512]{1,0:T(8,128)(2,1)S(1)}, u32[]{:S(2)}, u32[]{:S(2)}) %collective-permute-start.2) | collective-permute-done | bytes 65568 | tf_op jit(solution)/shard_map/ppermute | solution.py:246
  49.3 3.1 %collective-permute-start.3 = (bf16[256,512]{1,0:T(8,128)(2,1)S(1)}, bf16[256,512]{1,0:T(8,128)(2,1)S(1)}, u32[]{:S(2)}, u32[]{:S(2)}) collective-permute-start(bf16[256,512]{1,0:T(8,128)(2,1)S(1)} %constant_dynamic-update-slice_fusion.refs_0_), channel_id=1, source_target_pairs={{0,256},{64,320},{128,384},{192,448},{256,512},{320,576},{384,640}... | collective-permute-start | bytes 786440 | tf_op jit(solution)/shard_map/ppermute | solution.py:253
  52.5 3.4 %collective-permute-start.4 = (bf16[256,512]{1,0:T(8,128)(2,1)S(1)}, bf16[256,512]{1,0:T(8,128)(2,1)S(1)}, u32[]{:S(2)}, u32[]{:S(2)}) collective-permute-start(bf16[256,512]{1,0:T(8,128)(2,1)S(1)} %constant_dynamic-update-slice_fusion.refs_0_), channel_id=1, source_target_pairs={{0,768},{64,832},{128,896},{192,960},{256,0},{320,64},{384,128},{4... | collective-permute-start | bytes 786440 | tf_op jit(solution)/shard_map/ppermute | solution.py:253
  56.1 2.6 %collective-permute-done.3.refs_1_ = bf16[256,512]{1,0:T(8,128)(2,1)S(1)} collective-permute-done((bf16[256,512]{1,0:T(8,128)(2,1)S(1)}, bf16[256,512]{1,0:T(8,128)(2,1)S(1)}, u32[]{:S(2)}, u32[]{:S(2)}) %collective-permute-start.3) | collective-permute-done | bytes 262176 | tf_op jit(solution)/shard_map/ppermute | solution.py:253
  58.6 1.6 %collective-permute-done.4.refs_2_.refs_3_ = bf16[256,512]{1,0:T(8,128)(2,1)S(1)} collective-permute-done((bf16[256,512]{1,0:T(8,128)(2,1)S(1)}, bf16[256,512]{1,0:T(8,128)(2,1)S(1)}, u32[]{:S(2)}, u32[]{:S(2)}) %collective-permute-start.4) | collective-permute-done | bytes 262176 | tf_op jit(solution)/shard_map/ppermute | solution.py:253
  60.3 4.2 %all-to-all-done.arrived_ref = bf16[64,4,512]{2,1,0:T(4,128)(2,1)S(1)} async-done(((bf16[64,4,512]{2,1,0:T(4,128)(2,1)}), bf16[64,4,512]{2,1,0:T(4,128)(2,1)S(1)}, u32[]{:S(2)}, u32[]{:S(2)}) %all-to-all-start) | async-done | bytes 262176 | tf_op jit(solution)/shard_map/all_to_all | solution.py:229
  64.5 1.8 %shard_map.104 = (bf16[16,40,512]{2,1,0:T(8,128)(2,1)}, f32[4,8,4,512]{3,2,1,0:T(4,128)}) custom-call(s32[4]{0:T(128)S(1)} %select_reduce_fusion.band_ref, bf16[64,4,512]{2,1,0:T(4,128)(2,1)S(1)} %all-to-all-done.arrived_ref, f32[4,8,4,512]{3,2,1,0:T(4,128)S(1)} %bitcast.14, bf16[256,512]{1,0:T(8,128)(2,1)S(1)} %constant_dynamic-update-slice_fusion.refs_0_, ...), custom_call_target="tpu_custom_call" | custom-call | tf_op jit(solution)/shard_map/pallas_call | solution.py:256
  66.3 6.8 %all-to-all-start.1 = ((bf16[16,40,512]{2,1,0:T(8,128)(2,1)}), bf16[16,40,512]{2,1,0:T(8,128)(2,1)S(1)}, u32[]{:S(2)}, u32[]{:S(2)}) async-start(bf16[16,40,512]{2,1,0:T(8,128)(2,1)} %get-tuple-element.20), calls=%async_computation.1 | async-start | bytes 1310720 | tf_op jit(solution)/shard_map/all_to_all | solution.py:266
  73.1 4.8 %collective-permute-start.5 = (bf16[256,512]{1,0:T(8,128)(2,1)S(1)}, bf16[256,512]{1,0:T(8,128)(2,1)S(1)}, u32[]{:S(2)}, u32[]{:S(2)}) collective-permute-start(bf16[256,512]{1,0:T(8,128)(2,1)S(1)} %constant_dynamic-update-slice_fusion.refs_0_), channel_id=1, source_target_pairs={{0,512},{64,576},{128,640},{192,704},{256,768},{320,832},{384,896}... | collective-permute-start | bytes 786440 | tf_op jit(solution)/shard_map/ppermute | solution.py:253
  77.9 11.1 %collective-permute-done.5.refs_2_ = bf16[256,512]{1,0:T(8,128)(2,1)S(1)} collective-permute-done((bf16[256,512]{1,0:T(8,128)(2,1)S(1)}, bf16[256,512]{1,0:T(8,128)(2,1)S(1)}, u32[]{:S(2)}, u32[]{:S(2)}) %collective-permute-start.5) | collective-permute-done | bytes 262176 | tf_op jit(solution)/shard_map/ppermute | solution.py:253
  89.0 1.4 shard_map.105
  90.4 8.6 %all_to_all.20.back_ref = bf16[4,32,512]{2,1,0:T(8,128)(2,1)S(1)} all-to-all(bf16[4,32,512]{2,1,0:T(8,128)(2,1)S(1)} %shard_map.105), channel_id=1, replica_groups={{0,64,128,192},{256,320,384,448},{512,576,640,704},{768,832,896,960},{1..., dimensions={0} | all-to-all | bytes 262144 | tf_op jit(solution)/shard_map/all_to_all | solution.py:279
  99.0 1.5 shard_map.106._
  100.5 19.9 %all-to-all-start.3 = ((bf16[64,4,512]{2,1,0:T(4,128)(2,1)}), bf16[64,4,512]{2,1,0:T(4,128)(2,1)S(1)}, u32[]{:S(2)}, u32[]{:S(2)}) async-start(bf16[64,4,512]{2,1,0:T(4,128)(2,1)} %shard_map.106._), calls=%async_computation.3 | async-start | bytes 524288 | tf_op jit(solution)/shard_map/all_to_all | solution.py:289
  120.4 1.1 shard_map.108
  121.5 2.2 %collective-permute-start.6 = (bf16[64,512]{1,0:T(8,128)(2,1)S(1)}, bf16[64,512]{1,0:T(8,128)(2,1)S(1)}, u32[]{:S(2)}, u32[]{:S(2)}) collective-permute-start(bf16[64,512]{1,0:T(8,128)(2,1)S(1)} %get-tuple-element.22), channel_id=1, source_target_pairs={{0,64},{64,128},{128,192},{192,0},{256,320},{320,384},{384,448},{4... | collective-permute-start | bytes 196616 | tf_op jit(solution)/shard_map/ppermute | solution.py:246
  123.7 3.7 %collective-permute-start.7 = (bf16[64,512]{1,0:T(8,128)(2,1)S(1)}, bf16[64,512]{1,0:T(8,128)(2,1)S(1)}, u32[]{:S(2)}, u32[]{:S(2)}) collective-permute-start(bf16[64,512]{1,0:T(8,128)(2,1)S(1)} %get-tuple-element.23), channel_id=1, source_target_pairs={{0,128},{64,192},{128,0},{192,64},{256,384},{320,448},{384,256},{4... | collective-permute-start | bytes 196616 | tf_op jit(solution)/shard_map/ppermute | solution.py:246
  127.4 2.5 %collective-permute-start.8 = (bf16[64,512]{1,0:T(8,128)(2,1)S(1)}, bf16[64,512]{1,0:T(8,128)(2,1)S(1)}, u32[]{:S(2)}, u32[]{:S(2)}) collective-permute-start(bf16[64,512]{1,0:T(8,128)(2,1)S(1)} %get-tuple-element.24), channel_id=1, source_target_pairs={{0,192},{64,0},{128,64},{192,128},{256,448},{320,256},{384,320},{4... | collective-permute-start | bytes 196616 | tf_op jit(solution)/shard_map/ppermute | solution.py:246
  129.9 0.6 collective-permute-done.7.refs_2_
  130.5 2.2 %collective-permute-done.8.refs_3_ = bf16[64,512]{1,0:T(8,128)(2,1)S(1)} collective-permute-done((bf16[64,512]{1,0:T(8,128)(2,1)S(1)}, bf16[64,512]{1,0:T(8,128)(2,1)S(1)}, u32[]{:S(2)}, u32[]{:S(2)}) %collective-permute-start.8) | collective-permute-done | bytes 65568 | tf_op jit(solution)/shard_map/ppermute | solution.py:246
  132.7 0.9 shard_map.109
  133.6 16.4 %all-to-all-done.3.returned_ref = bf16[64,4,512]{2,1,0:T(4,128)(2,1)S(1)} async-done(((bf16[64,4,512]{2,1,0:T(4,128)(2,1)}), bf16[64,4,512]{2,1,0:T(4,128)(2,1)S(1)}, u32[]{:S(2)}, u32[]{:S(2)}) %all-to-all-start.3) | async-done | bytes 262176 | tf_op jit(solution)/shard_map/all_to_all | solution.py:289
  150.0 1.5 shard_map.107
  (27 shorter events, 0.5 us)
Async XLA Ops:
  0.6 0.7 copy-start.4
  1.3 0.9 copy-start.3
  3.7 31.2 %copy-start.5 = (bf16[1,4,8,1,4,512]{5,4,3,2,1,0:T(4,128)(2,1)S(1)}, bf16[1,4,8,1,4,512]{5,4,3,2,1,0:T(4,128)(2,1)}, u32[]{:S(2)}) copy-start(bf16[1,4,8,1,4,512]{5,4,3,2,1,0:T(4,128)(2,1)} %param.11) | copy-start | bytes 393220
  3.7 60.8 %all-to-all-start = ((bf16[64,4,512]{2,1,0:T(4,128)(2,1)}), bf16[64,4,512]{2,1,0:T(4,128)(2,1)S(1)}, u32[]{:S(2)}, u32[]{:S(2)}) async-start(bf16[64,4,512]{2,1,0:T(4,128)(2,1)} %shard_map.102), calls=%async_computation | async-start | bytes 524288 | tf_op jit(solution)/shard_map/all_to_all | solution.py:229
  34.9 0.9 copy-start.6
  36.3 10.8 %collective-permute-start = (bf16[64,512]{1,0:T(8,128)(2,1)S(1)}, bf16[64,512]{1,0:T(8,128)(2,1)S(1)}, u32[]{:S(2)}, u32[]{:S(2)}) collective-permute-start(bf16[64,512]{1,0:T(8,128)(2,1)S(1)} %get-tuple-element.17), channel_id=1, source_target_pairs={{0,64},{64,128},{128,192},{192,0},{256,320},{320,384},{384,448},{4... | collective-permute-start | bytes 196616 | tf_op jit(solution)/shard_map/ppermute | solution.py:246
  39.5 7.6 %collective-permute-start.1 = (bf16[64,512]{1,0:T(8,128)(2,1)S(1)}, bf16[64,512]{1,0:T(8,128)(2,1)S(1)}, u32[]{:S(2)}, u32[]{:S(2)}) collective-permute-start(bf16[64,512]{1,0:T(8,128)(2,1)S(1)} %get-tuple-element.18), channel_id=1, source_target_pairs={{0,128},{64,192},{128,0},{192,64},{256,384},{320,448},{384,256},{4... | collective-permute-start | bytes 196616 | tf_op jit(solution)/shard_map/ppermute | solution.py:246
  44.0 5.3 %collective-permute-start.2 = (bf16[64,512]{1,0:T(8,128)(2,1)S(1)}, bf16[64,512]{1,0:T(8,128)(2,1)S(1)}, u32[]{:S(2)}, u32[]{:S(2)}) collective-permute-start(bf16[64,512]{1,0:T(8,128)(2,1)S(1)} %get-tuple-element.19), channel_id=1, source_target_pairs={{0,192},{64,0},{128,64},{192,128},{256,448},{320,256},{384,320},{4... | collective-permute-start | bytes 196616 | tf_op jit(solution)/shard_map/ppermute | solution.py:246
  47.0 17.5 %copy-start = (f32[1,4,8,1,4,512]{5,4,3,2,1,0:T(4,128)S(1)}, f32[1,4,8,1,4,512]{5,4,3,2,1,0:T(4,128)}, u32[]{:S(2)}) copy-start(f32[1,4,8,1,4,512]{5,4,3,2,1,0:T(4,128)} %param.13) | copy-start | bytes 786436
  49.3 9.3 %collective-permute-start.3 = (bf16[256,512]{1,0:T(8,128)(2,1)S(1)}, bf16[256,512]{1,0:T(8,128)(2,1)S(1)}, u32[]{:S(2)}, u32[]{:S(2)}) collective-permute-start(bf16[256,512]{1,0:T(8,128)(2,1)S(1)} %constant_dynamic-update-slice_fusion.refs_0_), channel_id=1, source_target_pairs={{0,256},{64,320},{128,384},{192,448},{256,512},{320,576},{384,640}... | collective-permute-start | bytes 786440 | tf_op jit(solution)/shard_map/ppermute | solution.py:253
  52.5 7.8 %collective-permute-start.4 = (bf16[256,512]{1,0:T(8,128)(2,1)S(1)}, bf16[256,512]{1,0:T(8,128)(2,1)S(1)}, u32[]{:S(2)}, u32[]{:S(2)}) collective-permute-start(bf16[256,512]{1,0:T(8,128)(2,1)S(1)} %constant_dynamic-update-slice_fusion.refs_0_), channel_id=1, source_target_pairs={{0,768},{64,832},{128,896},{192,960},{256,0},{320,64},{384,128},{4... | collective-permute-start | bytes 786440 | tf_op jit(solution)/shard_map/ppermute | solution.py:253
  66.3 22.7 %all-to-all-start.1 = ((bf16[16,40,512]{2,1,0:T(8,128)(2,1)}), bf16[16,40,512]{2,1,0:T(8,128)(2,1)S(1)}, u32[]{:S(2)}, u32[]{:S(2)}) async-start(bf16[16,40,512]{2,1,0:T(8,128)(2,1)} %get-tuple-element.20), calls=%async_computation.1 | async-start | bytes 1310720 | tf_op jit(solution)/shard_map/all_to_all | solution.py:266
  73.1 15.9 %collective-permute-start.5 = (bf16[256,512]{1,0:T(8,128)(2,1)S(1)}, bf16[256,512]{1,0:T(8,128)(2,1)S(1)}, u32[]{:S(2)}, u32[]{:S(2)}) collective-permute-start(bf16[256,512]{1,0:T(8,128)(2,1)S(1)} %constant_dynamic-update-slice_fusion.refs_0_), channel_id=1, source_target_pairs={{0,512},{64,576},{128,640},{192,704},{256,768},{320,832},{384,896}... | collective-permute-start | bytes 786440 | tf_op jit(solution)/shard_map/ppermute | solution.py:253
  100.5 49.5 %all-to-all-start.3 = ((bf16[64,4,512]{2,1,0:T(4,128)(2,1)}), bf16[64,4,512]{2,1,0:T(4,128)(2,1)S(1)}, u32[]{:S(2)}, u32[]{:S(2)}) async-start(bf16[64,4,512]{2,1,0:T(4,128)(2,1)} %shard_map.106._), calls=%async_computation.3 | async-start | bytes 524288 | tf_op jit(solution)/shard_map/all_to_all | solution.py:289
  120.4 12.3 %copy-start.1 = (f32[1,4,8,1,4,512]{5,4,3,2,1,0:T(4,128)S(1)}, f32[1,4,8,1,4,512]{5,4,3,2,1,0:T(4,128)}, u32[]{:S(2)}) copy-start(f32[1,4,8,1,4,512]{5,4,3,2,1,0:T(4,128)} %param.9) | copy-start | bytes 786436
  120.4 12.3 %copy-start.2 = (f32[1,4,8,1,4,512]{5,4,3,2,1,0:T(4,128)S(1)}, f32[1,4,8,1,4,512]{5,4,3,2,1,0:T(4,128)}, u32[]{:S(2)}) copy-start(f32[1,4,8,1,4,512]{5,4,3,2,1,0:T(4,128)} %param.10) | copy-start | bytes 786436
  121.5 8.4 %collective-permute-start.6 = (bf16[64,512]{1,0:T(8,128)(2,1)S(1)}, bf16[64,512]{1,0:T(8,128)(2,1)S(1)}, u32[]{:S(2)}, u32[]{:S(2)}) collective-permute-start(bf16[64,512]{1,0:T(8,128)(2,1)S(1)} %get-tuple-element.22), channel_id=1, source_target_pairs={{0,64},{64,128},{128,192},{192,0},{256,320},{320,384},{384,448},{4... | collective-permute-start | bytes 196616 | tf_op jit(solution)/shard_map/ppermute | solution.py:246
  123.7 6.8 %collective-permute-start.7 = (bf16[64,512]{1,0:T(8,128)(2,1)S(1)}, bf16[64,512]{1,0:T(8,128)(2,1)S(1)}, u32[]{:S(2)}, u32[]{:S(2)}) collective-permute-start(bf16[64,512]{1,0:T(8,128)(2,1)S(1)} %get-tuple-element.23), channel_id=1, source_target_pairs={{0,128},{64,192},{128,0},{192,64},{256,384},{320,448},{384,256},{4... | collective-permute-start | bytes 196616 | tf_op jit(solution)/shard_map/ppermute | solution.py:246
  127.4 5.3 %collective-permute-start.8 = (bf16[64,512]{1,0:T(8,128)(2,1)S(1)}, bf16[64,512]{1,0:T(8,128)(2,1)S(1)}, u32[]{:S(2)}, u32[]{:S(2)}) collective-permute-start(bf16[64,512]{1,0:T(8,128)(2,1)S(1)} %get-tuple-element.24), channel_id=1, source_target_pairs={{0,192},{64,0},{128,64},{192,128},{256,448},{320,256},{384,320},{4... | collective-permute-start | bytes 196616 | tf_op jit(solution)/shard_map/ppermute | solution.py:246

commit v3 on v2

--- a/solution.py
+++ b/solution.py
@@ -19,18 +19,19 @@
 
 
 ORDER_STEP = 31
-ORDER_FIRST = 22
-
-
-def place_of(owner, owners):
+FIRST_OUT = 22
+FIRST_BACK = 14
+
+
+def place_of(owner, owners, first):
     half = owners // 2
     back = pow(ORDER_STEP, -1, half)
-    return lax.rem(owner, 2) * half + lax.rem((owner // 2 + half - ORDER_FIRST) * back, half)
-
-
-def exchange_order(owners):
+    return lax.rem(owner, 2) * half + lax.rem((owner // 2 + half - first) * back, half)
+
+
+def exchange_order(owners, first):
     half = owners // 2
-    chips = [(ORDER_FIRST + i * ORDER_STEP) % half for i in range(half)]
+    chips = [(first + i * ORDER_STEP) % half for i in range(half)]
     return [[2 * chip + core for core in range(2) for chip in chips]]
 
 
@@ -45,6 +46,12 @@
     )
 
 
+def exchange(array, axis, groups=None):
+    return lax.all_to_all(
+        array, axis, split_axis=0, concat_axis=0, tiled=True, axis_index_groups=groups
+    )
+
+
 def dot(a, b, contract=(1, 0)):
     return lax.dot_general(
         a, b, (((contract[0],), (contract[1],)), ((), ())), preferred_element_type=jnp.float32
@@ -57,7 +64,7 @@
     band = lax.axis_index("fsdp") // shards
     for column in range(count):
         owner = owner_ref[band * count + column]
-        out_ref[place_of(owner, out_ref.shape[0])] = grad_ref[:, column * width : (column + 1) * width]
+        out_ref[place_of(owner, out_ref.shape[0], FIRST_OUT)] = grad_ref[:, column * width : (column + 1) * width]
 
 
 def own_rows_kernel(band_ref, arrived_ref, moment_ref, *refs):
@@ -70,7 +77,7 @@
         band = band_ref[slot]
         total = jnp.zeros((dev_rows, width), jnp.float32)
         for shard in range(shards):
-            values = arrived_ref[place_of(band * shards + shard, owners)].astype(jnp.float32)
+            values = arrived_ref[place_of(band * shards + shard, owners, FIRST_OUT)].astype(jnp.float32)
             moment = (
                 MOMENT_DECAY * moment_ref[slot, shard] + (1.0 - MOMENT_DECAY) * values * values
             )
@@ -159,7 +166,7 @@
     for slot in range(back_ref.shape[0]):
         band = band_ref[slot]
         for shard in range(shards):
-            out_ref[place_of(band * shards + shard, out_ref.shape[0])] = back_ref[
+            out_ref[place_of(band * shards + shard, out_ref.shape[0], FIRST_BACK)] = back_ref[
                 slot, shard * dev_rows : (shard + 1) * dev_rows, :
             ]
 
@@ -171,7 +178,7 @@
     for column in range(count):
         owner = owner_ref[band * count + column]
         out_ref[:, column * width : (column + 1) * width] = returned_ref[
-            place_of(owner, returned_ref.shape[0])
+            place_of(owner, returned_ref.shape[0], FIRST_BACK)
         ]
 
 
@@ -216,7 +223,8 @@
     rows = shards * dev_rows
     columns = columns_all // width
     groups = [list(range(i, i + slots)) for i in range(0, replicas, slots)]
-    turns = exchange_order(owners)
+    out_turns = exchange_order(owners, FIRST_OUT)
+    back_turns = exchange_order(owners, FIRST_BACK)
     pieces = (owners, dev_rows, width)
     by_piece = (slots, shards, dev_rows, width)
 
@@ -226,7 +234,7 @@
         [SMEM, VMEM],
         VMEM,
     )(block_owner, grad.reshape(dev_rows, columns_all))
-    arrived = lax.all_to_all(outgoing, "fsdp", split_axis=0, concat_axis=0, tiled=True, axis_index_groups=turns)
+    arrived = exchange(outgoing, "fsdp", out_turns)
 
     bands = owned_bands(block_owner, lax.axis_index("fsdp"), slots, columns)
     order = device_order(shards, replicas, dev_rows)
@@ -252,17 +260,16 @@
         pairs = [(i * slots + j, (i + step) % lines * slots + j) for i, j in devices]
         roots.append(lax.ppermute(line_roots, "dp", pairs))
 
-    early = roots[:2] + roots[3:]
     packed, moment_new = call(
         own_rows_kernel,
         (
             jax.ShapeDtypeStruct((replicas, rows + NORM_ROWS, width), jnp.bfloat16),
             jax.ShapeDtypeStruct(by_piece, jnp.float32),
         ),
-        [SMEM, VMEM, VMEM] + [ANY] * len(early),
+        [SMEM, VMEM, VMEM] + [ANY] * len(roots),
         (VMEM, VMEM),
         [pltpu.VMEM((rows, width), jnp.float32)],
-    )(bands, arrived, moment.reshape(by_piece), *early)
+    )(bands, arrived, moment.reshape(by_piece), *roots)
     gathered = lax.all_to_all(packed, "dp", split_axis=0, concat_axis=0, tiled=True)
 
     results = call(
@@ -286,7 +293,7 @@
         [SMEM, VMEM],
         VMEM,
     )(bands, back)
-    returned = lax.all_to_all(returning, "fsdp", split_axis=0, concat_axis=0, tiled=True, axis_index_groups=turns)
+    returned = exchange(returning, "fsdp", back_turns)
 
     own_grams, *grams = call(
         functools.partial(gram_kernel, rows),

time: 152 us -> 149 us (0.980)
  blocking collectives: 8.59 us -> 21.3 us
  waiting for transfers between devices: 41 us -> 29.1 us
  starting transfers between devices: 88.2 us -> 84.1 us
    all_to_all x0 -> x1, blocking collectives: none -> 14.1 us  [body(): lax.all_to_all(packed, 'dp', split_axis=0, concat_axis=0, tiled=True)]
    all_to_all x3 -> x2, waiting for transfers between devices: 20.6 us -> 12.8 us  [exchange(): lax.all_to_all(array, axis, split_axis=0, concat_axis=0, tiled=True, axis...]
    ppermute x3, waiting for transfers between devices: 15.3 us -> 11.3 us  [body(): roots.append(lax.ppermute(line_roots, 'dp', pairs))]
    all_to_all x3 -> x2, starting transfers between devices: 57.8 us -> 55.6 us  [exchange(): lax.all_to_all(array, axis, split_axis=0, concat_axis=0, tiled=True, axis...]
    ppermute x3, starting transfers between devices: 11.3 us -> 9.32 us  [body(): roots.append(lax.ppermute(line_roots, 'dp', pairs))]
  transfers between devices with their start and end apart: 12 -> 11, of which waited for: 8 -> 6; matrix products, arithmetic and copies ran while one was open for 0% -> 0% of each run, Pallas kernels for 1% -> 1%
where the time goes in v3:
time: 149 us; the launch traced here: 148 us
  starting transfers between devices  84.1 us (56%)
  waiting for transfers between devices  29.1 us (20%)
  blocking collectives  21.3 us (14%)
  Pallas kernels  9.58 us (6%)
  local copies, waits for them, and re-layouts  2.56 us (2%)
    all_to_all x2, starting transfers between devices, exchange(): lax.all_to_all(array, axis, split_axis=0, concat_axis=0, tiled=True, axis...  55.6 us
    ppermute x6, starting transfers between devices, along_line(): return lax.ppermute(part, 'dp', pairs)  19.1 us
    all_to_all x1, blocking collectives, body(): lax.all_to_all(packed, 'dp', split_axis=0, concat_axis=0, tiled=True)  14.1 us
    all_to_all x2, waiting for transfers between devices, exchange(): lax.all_to_all(array, axis, split_axis=0, concat_axis=0, tiled=True, axis...  12.8 us
    ppermute x3, waiting for transfers between devices, body(): roots.append(lax.ppermute(line_roots, 'dp', pairs))  11.3 us
    ppermute x3, starting transfers between devices, body(): roots.append(lax.ppermute(line_roots, 'dp', pairs))  9.32 us
    all_to_all x1, blocking collectives, body(): lax.all_to_all(results, 'dp', split_axis=0, concat_axis=0, tiled=True, ax...  7.21 us
    ppermute x6, waiting for transfers between devices, along_line(): return lax.ppermute(part, 'dp', pairs)  4.99 us
  transfers between devices with their start and end apart: 11, of which 6 were waited for; matrix products, arithmetic and copies ran while one was open for 0% of the time, Pallas kernels for 1%

profile of v3, /device:TPU:1, one launch (start us, length us, event | category | flops | bytes accessed | tf_op | source)
XLA Modules:
  0.0 147.9 jit_solution(6504270194197467526)
XLA Ops:
  0.6 0.7 copy-done.4
  1.3 0.9 copy-done.3
  2.2 1.5 %shard_map.102 = bf16[64,4,512]{2,1,0:T(4,128)(2,1)} custom-call(s32[256]{0:T(256)S(1)} %copy-done.4, bf16[4,16384]{1,0:T(4,128)(2,1)S(1)} %bitcast.17), custom_call_target="tpu_custom_call" | custom-call | tf_op jit(solution)/shard_map/pallas_call | solution.py:231
  3.7 31.2 %all-to-all-start = ((bf16[64,4,512]{2,1,0:T(4,128)(2,1)}), bf16[64,4,512]{2,1,0:T(4,128)(2,1)S(1)}, u32[]{:S(2)}, u32[]{:S(2)}) async-start(bf16[64,4,512]{2,1,0:T(4,128)(2,1)} %shard_map.102), calls=%async_computation | async-start | bytes 524288 | tf_op jit(solution)/shard_map/all_to_all | solution.py:50
  35.0 0.9 copy-done.6
  35.9 0.1 fusion.order_ref
  36.0 0.2 shard_map.103
  36.3 3.2 %collective-permute-start = (bf16[64,512]{1,0:T(8,128)(2,1)S(1)}, bf16[64,512]{1,0:T(8,128)(2,1)S(1)}, u32[]{:S(2)}, u32[]{:S(2)}) collective-permute-start(bf16[64,512]{1,0:T(8,128)(2,1)S(1)} %get-tuple-element.17), channel_id=1, source_target_pairs={{0,64},{64,128},{128,192},{192,0},{256,320},{320,384},{384,448},{4... | collective-permute-start | bytes 196616 | tf_op jit(solution)/shard_map/ppermute | solution.py:254
  39.5 4.5 %collective-permute-start.1 = (bf16[64,512]{1,0:T(8,128)(2,1)S(1)}, bf16[64,512]{1,0:T(8,128)(2,1)S(1)}, u32[]{:S(2)}, u32[]{:S(2)}) collective-permute-start(bf16[64,512]{1,0:T(8,128)(2,1)S(1)} %get-tuple-element.18), channel_id=1, source_target_pairs={{0,128},{64,192},{128,0},{192,64},{256,384},{320,448},{384,256},{4... | collective-permute-start | bytes 196616 | tf_op jit(solution)/shard_map/ppermute | solution.py:254
  44.0 3.0 %collective-permute-start.2 = (bf16[64,512]{1,0:T(8,128)(2,1)S(1)}, bf16[64,512]{1,0:T(8,128)(2,1)S(1)}, u32[]{:S(2)}, u32[]{:S(2)}) collective-permute-start(bf16[64,512]{1,0:T(8,128)(2,1)S(1)} %get-tuple-element.19), channel_id=1, source_target_pairs={{0,192},{64,0},{128,64},{192,128},{256,448},{320,256},{384,320},{4... | collective-permute-start | bytes 196616 | tf_op jit(solution)/shard_map/ppermute | solution.py:254
  47.1 2.2 %collective-permute-done.2 = bf16[64,512]{1,0:T(8,128)(2,1)S(1)} collective-permute-done((bf16[64,512]{1,0:T(8,128)(2,1)S(1)}, bf16[64,512]{1,0:T(8,128)(2,1)S(1)}, u32[]{:S(2)}, u32[]{:S(2)}) %collective-permute-start.2) | collective-permute-done | bytes 65568 | tf_op jit(solution)/shard_map/ppermute | solution.py:254
  49.3 4.4 %collective-permute-start.5 = (bf16[256,512]{1,0:T(8,128)(2,1)S(1)}, bf16[256,512]{1,0:T(8,128)(2,1)S(1)}, u32[]{:S(2)}, u32[]{:S(2)}) collective-permute-start(bf16[256,512]{1,0:T(8,128)(2,1)S(1)} %constant_dynamic-update-slice_fusion.refs_0_), channel_id=1, source_target_pairs={{0,768},{64,832},{128,896},{192,960},{256,0},{320,64},{384,128},{4... | collective-permute-start | bytes 786440 | tf_op jit(solution)/shard_map/ppermute | solution.py:261
  53.7 2.4 %collective-permute-start.4 = (bf16[256,512]{1,0:T(8,128)(2,1)S(1)}, bf16[256,512]{1,0:T(8,128)(2,1)S(1)}, u32[]{:S(2)}, u32[]{:S(2)}) collective-permute-start(bf16[256,512]{1,0:T(8,128)(2,1)S(1)} %constant_dynamic-update-slice_fusion.refs_0_), channel_id=1, source_target_pairs={{0,512},{64,576},{128,640},{192,704},{256,768},{320,832},{384,896}... | collective-permute-start | bytes 786440 | tf_op jit(solution)/shard_map/ppermute | solution.py:261
  56.2 2.5 %collective-permute-start.3 = (bf16[256,512]{1,0:T(8,128)(2,1)S(1)}, bf16[256,512]{1,0:T(8,128)(2,1)S(1)}, u32[]{:S(2)}, u32[]{:S(2)}) collective-permute-start(bf16[256,512]{1,0:T(8,128)(2,1)S(1)} %constant_dynamic-update-slice_fusion.refs_0_), channel_id=1, source_target_pairs={{0,256},{64,320},{128,384},{192,448},{256,512},{320,576},{384,640}... | collective-permute-start | bytes 786440 | tf_op jit(solution)/shard_map/ppermute | solution.py:261
  58.8 0.1 select_reduce_fusion.band_ref
  58.9 4.1 %collective-permute-done.4.refs_2_ = bf16[256,512]{1,0:T(8,128)(2,1)S(1)} collective-permute-done((bf16[256,512]{1,0:T(8,128)(2,1)S(1)}, bf16[256,512]{1,0:T(8,128)(2,1)S(1)}, u32[]{:S(2)}, u32[]{:S(2)}) %collective-permute-start.4) | collective-permute-done | bytes 262176 | tf_op jit(solution)/shard_map/ppermute | solution.py:261
  63.0 7.2 %collective-permute-done.3.refs_1_ = bf16[256,512]{1,0:T(8,128)(2,1)S(1)} collective-permute-done((bf16[256,512]{1,0:T(8,128)(2,1)S(1)}, bf16[256,512]{1,0:T(8,128)(2,1)S(1)}, u32[]{:S(2)}, u32[]{:S(2)}) %collective-permute-start.3) | collective-permute-done | bytes 262176 | tf_op jit(solution)/shard_map/ppermute | solution.py:261
  70.2 1.5 %shard_map.104 = (bf16[16,40,512]{2,1,0:T(8,128)(2,1)S(1)}, f32[4,8,4,512]{3,2,1,0:T(4,128)}) custom-call(s32[4]{0:T(128)S(1)} %select_reduce_fusion.band_ref, bf16[64,4,512]{2,1,0:T(4,128)(2,1)S(1)} %all-to-all-done.arrived_ref, f32[4,8,4,512]{3,2,1,0:T(4,128)S(1)} %bitcast.16, bf16[256,512]{1,0:T(8,128)(2,1)S(1)} %constant_dynamic-update-slice_fusion.refs_0_, ...), custom_call_target="tpu_custom_call" | custom-call | tf_op jit(solution)/shard_map/pallas_call | solution.py:263
  71.7 14.1 %all_to_all.20.arrived_ref = bf16[16,40,512]{2,1,0:T(8,128)(2,1)S(1)} all-to-all(bf16[16,40,512]{2,1,0:T(8,128)(2,1)S(1)} %get-tuple-element.20), channel_id=1, replica_groups=mesh['dp'=16,'fsdp'=64] {'dp'}, dimensions={0} | all-to-all | bytes 1310720 | tf_op jit(solution)/shard_map/all_to_all | solution.py:273
  85.9 1.4 shard_map.105
  87.3 7.2 %all_to_all.21.back_ref = bf16[4,32,512]{2,1,0:T(8,128)(2,1)S(1)} all-to-all(bf16[4,32,512]{2,1,0:T(8,128)(2,1)S(1)} %shard_map.105), channel_id=1, replica_groups={{0,64,128,192},{256,320,384,448},{512,576,640,704},{768,832,896,960},{1..., dimensions={0} | all-to-all | bytes 262144 | tf_op jit(solution)/shard_map/all_to_all | solution.py:286
  94.5 1.5 %shard_map.106._ = bf16[64,4,512]{2,1,0:T(4,128)(2,1)} custom-call(s32[4]{0:T(128)S(1)} %select_reduce_fusion.band_ref, bf16[4,32,512]{2,1,0:T(8,128)(2,1)S(1)} %all_to_all.21.back_ref), custom_call_target="tpu_custom_call" | custom-call | tf_op jit(solution)/shard_map/pallas_call | solution.py:290
  96.0 24.5 %all-to-all-start.3 = ((bf16[64,4,512]{2,1,0:T(4,128)(2,1)}), bf16[64,4,512]{2,1,0:T(4,128)(2,1)S(1)}, u32[]{:S(2)}, u32[]{:S(2)}) async-start(bf16[64,4,512]{2,1,0:T(4,128)(2,1)} %shard_map.106._), calls=%async_computation.3 | async-start | bytes 524288 | tf_op jit(solution)/shard_map/all_to_all | solution.py:50
  120.5 1.1 shard_map.108
  121.5 2.2 %collective-permute-start.6 = (bf16[64,512]{1,0:T(8,128)(2,1)S(1)}, bf16[64,512]{1,0:T(8,128)(2,1)S(1)}, u32[]{:S(2)}, u32[]{:S(2)}) collective-permute-start(bf16[64,512]{1,0:T(8,128)(2,1)S(1)} %get-tuple-element.22), channel_id=1, source_target_pairs={{0,64},{64,128},{128,192},{192,0},{256,320},{320,384},{384,448},{4... | collective-permute-start | bytes 196616 | tf_op jit(solution)/shard_map/ppermute | solution.py:254
  123.7 3.7 %collective-permute-start.7 = (bf16[64,512]{1,0:T(8,128)(2,1)S(1)}, bf16[64,512]{1,0:T(8,128)(2,1)S(1)}, u32[]{:S(2)}, u32[]{:S(2)}) collective-permute-start(bf16[64,512]{1,0:T(8,128)(2,1)S(1)} %get-tuple-element.23), channel_id=1, source_target_pairs={{0,128},{64,192},{128,0},{192,64},{256,384},{320,448},{384,256},{4... | collective-permute-start | bytes 196616 | tf_op jit(solution)/shard_map/ppermute | solution.py:254
  127.4 2.5 %collective-permute-start.8 = (bf16[64,512]{1,0:T(8,128)(2,1)S(1)}, bf16[64,512]{1,0:T(8,128)(2,1)S(1)}, u32[]{:S(2)}, u32[]{:S(2)}) collective-permute-start(bf16[64,512]{1,0:T(8,128)(2,1)S(1)} %get-tuple-element.24), channel_id=1, source_target_pairs={{0,192},{64,0},{128,64},{192,128},{256,448},{320,256},{384,320},{4... | collective-permute-start | bytes 196616 | tf_op jit(solution)/shard_map/ppermute | solution.py:254
  130.0 0.6 collective-permute-done.7.refs_2_
  130.5 2.2 %collective-permute-done.8.refs_3_ = bf16[64,512]{1,0:T(8,128)(2,1)S(1)} collective-permute-done((bf16[64,512]{1,0:T(8,128)(2,1)S(1)}, bf16[64,512]{1,0:T(8,128)(2,1)S(1)}, u32[]{:S(2)}, u32[]{:S(2)}) %collective-permute-start.8) | collective-permute-done | bytes 65568 | tf_op jit(solution)/shard_map/ppermute | solution.py:254
  132.7 0.9 shard_map.109
  133.6 12.8 %all-to-all-done.3.returned_ref = bf16[64,4,512]{2,1,0:T(4,128)(2,1)S(1)} async-done(((bf16[64,4,512]{2,1,0:T(4,128)(2,1)}), bf16[64,4,512]{2,1,0:T(4,128)(2,1)S(1)}, u32[]{:S(2)}, u32[]{:S(2)}) %all-to-all-start.3) | async-done | bytes 262176 | tf_op jit(solution)/shard_map/all_to_all | solution.py:50
  146.4 1.5 shard_map.107
  (26 shorter events, 0.3 us)
Async XLA Ops:
  0.6 0.7 copy-start.4
  1.3 0.9 copy-start.3
  3.7 31.2 %copy-start.5 = (bf16[1,4,8,1,4,512]{5,4,3,2,1,0:T(4,128)(2,1)S(1)}, bf16[1,4,8,1,4,512]{5,4,3,2,1,0:T(4,128)(2,1)}, u32[]{:S(2)}) copy-start(bf16[1,4,8,1,4,512]{5,4,3,2,1,0:T(4,128)(2,1)} %param.11) | copy-start | bytes 393220
  3.7 66.5 %all-to-all-start = ((bf16[64,4,512]{2,1,0:T(4,128)(2,1)}), bf16[64,4,512]{2,1,0:T(4,128)(2,1)S(1)}, u32[]{:S(2)}, u32[]{:S(2)}) async-start(bf16[64,4,512]{2,1,0:T(4,128)(2,1)} %shard_map.102), calls=%async_computation | async-start | bytes 524288 | tf_op jit(solution)/shard_map/all_to_all | solution.py:50
  34.9 0.9 copy-start.6
  36.3 10.8 %collective-permute-start = (bf16[64,512]{1,0:T(8,128)(2,1)S(1)}, bf16[64,512]{1,0:T(8,128)(2,1)S(1)}, u32[]{:S(2)}, u32[]{:S(2)}) collective-permute-start(bf16[64,512]{1,0:T(8,128)(2,1)S(1)} %get-tuple-element.17), channel_id=1, source_target_pairs={{0,64},{64,128},{128,192},{192,0},{256,320},{320,384},{384,448},{4... | collective-permute-start | bytes 196616 | tf_op jit(solution)/shard_map/ppermute | solution.py:254
  39.5 7.6 %collective-permute-start.1 = (bf16[64,512]{1,0:T(8,128)(2,1)S(1)}, bf16[64,512]{1,0:T(8,128)(2,1)S(1)}, u32[]{:S(2)}, u32[]{:S(2)}) collective-permute-start(bf16[64,512]{1,0:T(8,128)(2,1)S(1)} %get-tuple-element.18), channel_id=1, source_target_pairs={{0,128},{64,192},{128,0},{192,64},{256,384},{320,448},{384,256},{4... | collective-permute-start | bytes 196616 | tf_op jit(solution)/shard_map/ppermute | solution.py:254
  44.0 5.3 %collective-permute-start.2 = (bf16[64,512]{1,0:T(8,128)(2,1)S(1)}, bf16[64,512]{1,0:T(8,128)(2,1)S(1)}, u32[]{:S(2)}, u32[]{:S(2)}) collective-permute-start(bf16[64,512]{1,0:T(8,128)(2,1)S(1)} %get-tuple-element.19), channel_id=1, source_target_pairs={{0,192},{64,0},{128,64},{192,128},{256,448},{320,256},{384,320},{4... | collective-permute-start | bytes 196616 | tf_op jit(solution)/shard_map/ppermute | solution.py:254
  47.0 23.2 %copy-start.2 = (f32[1,4,8,1,4,512]{5,4,3,2,1,0:T(4,128)S(1)}, f32[1,4,8,1,4,512]{5,4,3,2,1,0:T(4,128)}, u32[]{:S(2)}) copy-start(f32[1,4,8,1,4,512]{5,4,3,2,1,0:T(4,128)} %param.13) | copy-start | bytes 786436
  49.3 9.6 %collective-permute-start.5 = (bf16[256,512]{1,0:T(8,128)(2,1)S(1)}, bf16[256,512]{1,0:T(8,128)(2,1)S(1)}, u32[]{:S(2)}, u32[]{:S(2)}) collective-permute-start(bf16[256,512]{1,0:T(8,128)(2,1)S(1)} %constant_dynamic-update-slice_fusion.refs_0_), channel_id=1, source_target_pairs={{0,768},{64,832},{128,896},{192,960},{256,0},{320,64},{384,128},{4... | collective-permute-start | bytes 786440 | tf_op jit(solution)/shard_map/ppermute | solution.py:261
  53.7 9.3 %collective-permute-start.4 = (bf16[256,512]{1,0:T(8,128)(2,1)S(1)}, bf16[256,512]{1,0:T(8,128)(2,1)S(1)}, u32[]{:S(2)}, u32[]{:S(2)}) collective-permute-start(bf16[256,512]{1,0:T(8,128)(2,1)S(1)} %constant_dynamic-update-slice_fusion.refs_0_), channel_id=1, source_target_pairs={{0,512},{64,576},{128,640},{192,704},{256,768},{320,832},{384,896}... | collective-permute-start | bytes 786440 | tf_op jit(solution)/shard_map/ppermute | solution.py:261
  56.2 14.1 %collective-permute-start.3 = (bf16[256,512]{1,0:T(8,128)(2,1)S(1)}, bf16[256,512]{1,0:T(8,128)(2,1)S(1)}, u32[]{:S(2)}, u32[]{:S(2)}) collective-permute-start(bf16[256,512]{1,0:T(8,128)(2,1)S(1)} %constant_dynamic-update-slice_fusion.refs_0_), channel_id=1, source_target_pairs={{0,256},{64,320},{128,384},{192,448},{256,512},{320,576},{384,640}... | collective-permute-start | bytes 786440 | tf_op jit(solution)/shard_map/ppermute | solution.py:261
  96.0 50.5 %all-to-all-start.3 = ((bf16[64,4,512]{2,1,0:T(4,128)(2,1)}), bf16[64,4,512]{2,1,0:T(4,128)(2,1)S(1)}, u32[]{:S(2)}, u32[]{:S(2)}) async-start(bf16[64,4,512]{2,1,0:T(4,128)(2,1)} %shard_map.106._), calls=%async_computation.3 | async-start | bytes 524288 | tf_op jit(solution)/shard_map/all_to_all | solution.py:50
  120.4 12.3 %copy-start = (f32[1,4,8,1,4,512]{5,4,3,2,1,0:T(4,128)S(1)}, f32[1,4,8,1,4,512]{5,4,3,2,1,0:T(4,128)}, u32[]{:S(2)}) copy-start(f32[1,4,8,1,4,512]{5,4,3,2,1,0:T(4,128)} %param.9) | copy-start | bytes 786436
  120.4 12.3 %copy-start.1 = (f32[1,4,8,1,4,512]{5,4,3,2,1,0:T(4,128)S(1)}, f32[1,4,8,1,4,512]{5,4,3,2,1,0:T(4,128)}, u32[]{:S(2)}) copy-start(f32[1,4,8,1,4,512]{5,4,3,2,1,0:T(4,128)} %param.10) | copy-start | bytes 786436
  121.5 8.4 %collective-permute-start.6 = (bf16[64,512]{1,0:T(8,128)(2,1)S(1)}, bf16[64,512]{1,0:T(8,128)(2,1)S(1)}, u32[]{:S(2)}, u32[]{:S(2)}) collective-permute-start(bf16[64,512]{1,0:T(8,128)(2,1)S(1)} %get-tuple-element.22), channel_id=1, source_target_pairs={{0,64},{64,128},{128,192},{192,0},{256,320},{320,384},{384,448},{4... | collective-permute-start | bytes 196616 | tf_op jit(solution)/shard_map/ppermute | solution.py:254
  123.7 6.8 %collective-permute-start.7 = (bf16[64,512]{1,0:T(8,128)(2,1)S(1)}, bf16[64,512]{1,0:T(8,128)(2,1)S(1)}, u32[]{:S(2)}, u32[]{:S(2)}) collective-permute-start(bf16[64,512]{1,0:T(8,128)(2,1)S(1)} %get-tuple-element.23), channel_id=1, source_target_pairs={{0,128},{64,192},{128,0},{192,64},{256,384},{320,448},{384,256},{4... | collective-permute-start | bytes 196616 | tf_op jit(solution)/shard_map/ppermute | solution.py:254
  127.4 5.3 %collective-permute-start.8 = (bf16[64,512]{1,0:T(8,128)(2,1)S(1)}, bf16[64,512]{1,0:T(8,128)(2,1)S(1)}, u32[]{:S(2)}, u32[]{:S(2)}) collective-permute-start(bf16[64,512]{1,0:T(8,128)(2,1)S(1)} %get-tuple-element.24), channel_id=1, source_target_pairs={{0,192},{64,0},{128,64},{192,128},{256,448},{320,256},{384,320},{4... | collective-permute-start | bytes 196616 | tf_op jit(solution)/shard_map/ppermute | solution.py:254

commit v4 on v3

--- a/solution.py
+++ b/solution.py
@@ -19,14 +19,14 @@
 
 
 ORDER_STEP = 31
-FIRST_OUT = 22
-FIRST_BACK = 14
+FIRST_OUT = 24
+FIRST_BACK = 16
 
 
 def place_of(owner, owners, first):
     half = owners // 2
     back = pow(ORDER_STEP, -1, half)
-    return lax.rem(owner, 2) * half + lax.rem((owner // 2 + half - first) * back, half)
+    return (owner & 1) * half + ((((owner >> 1) - first) * back) & (half - 1))
 
 
 def exchange_order(owners, first):

time: 149 us -> 147 us (0.987)
  waiting for transfers between devices: 29.1 us -> 25.8 us
  starting transfers between devices: 84.1 us -> 85.6 us
    all_to_all x2, waiting for transfers between devices: 12.8 us -> 9.56 us  [exchange(): lax.all_to_all(array, axis, split_axis=0, concat_axis=0, tiled=True, axis...]
  transfers between devices with their start and end apart: 11 -> 11, of which waited for: 6 -> 6; matrix products, arithmetic and copies ran while one was open for 0% -> 0% of each run, Pallas kernels for 1% -> 2%
where the time goes in v4:
time: 147 us
  starting transfers between devices  85.6 us (58%)
  waiting for transfers between devices  25.8 us (18%)
  blocking collectives  22.7 us (15%)
  Pallas kernels  8.99 us (6%)
  local copies, waits for them, and re-layouts  2.56 us (2%)
    all_to_all x2, starting transfers between devices, exchange(): lax.all_to_all(array, axis, split_axis=0, concat_axis=0, tiled=True, axis...  57.1 us
    ppermute x6, starting transfers between devices, along_line(): return lax.ppermute(part, 'dp', pairs)  19.1 us
    all_to_all x1, blocking collectives, body(): lax.all_to_all(packed, 'dp', split_axis=0, concat_axis=0, tiled=True)  15.1 us
    ppermute x3, waiting for transfers between devices, body(): roots.append(lax.ppermute(line_roots, 'dp', pairs))  11.3 us
    all_to_all x2, waiting for transfers between devices, exchange(): lax.all_to_all(array, axis, split_axis=0, concat_axis=0, tiled=True, axis...  9.56 us
    ppermute x3, starting transfers between devices, body(): roots.append(lax.ppermute(line_roots, 'dp', pairs))  9.32 us
    all_to_all x1, blocking collectives, body(): lax.all_to_all(results, 'dp', split_axis=0, concat_axis=0, tiled=True, ax...  7.61 us
    ppermute x6, waiting for transfers between devices, along_line(): return lax.ppermute(part, 'dp', pairs)  4.99 us
  transfers between devices with their start and end apart: 11, of which 6 were waited for; matrix products, arithmetic and copies ran while one was open for 0% of the time, Pallas kernels for 2%

profile of v4, /device:TPU:1, one launch (start us, length us, event | category | flops | bytes accessed | tf_op | source)
XLA Modules:
  0.0 146.9 jit_solution(12251328682767291146)
XLA Ops:
  0.6 0.7 copy-done.4
  1.3 0.9 copy-done.3
  2.2 1.4 shard_map.102
  3.6 31.0 %all-to-all-start = ((bf16[64,4,512]{2,1,0:T(4,128)(2,1)}), bf16[64,4,512]{2,1,0:T(4,128)(2,1)S(1)}, u32[]{:S(2)}, u32[]{:S(2)}) async-start(bf16[64,4,512]{2,1,0:T(4,128)(2,1)} %shard_map.102), calls=%async_computation | async-start | bytes 524288 | tf_op jit(solution)/shard_map/all_to_all | solution.py:50
  34.6 0.9 copy-done.6
  35.5 0.1 fusion.order_ref
  35.7 0.2 shard_map.103
  35.9 3.2 %collective-permute-start = (bf16[64,512]{1,0:T(8,128)(2,1)S(1)}, bf16[64,512]{1,0:T(8,128)(2,1)S(1)}, u32[]{:S(2)}, u32[]{:S(2)}) collective-permute-start(bf16[64,512]{1,0:T(8,128)(2,1)S(1)} %get-tuple-element.17), channel_id=1, source_target_pairs={{0,64},{64,128},{128,192},{192,0},{256,320},{320,384},{384,448},{4... | collective-permute-start | bytes 196616 | tf_op jit(solution)/shard_map/ppermute | solution.py:254
  39.1 4.5 %collective-permute-start.1 = (bf16[64,512]{1,0:T(8,128)(2,1)S(1)}, bf16[64,512]{1,0:T(8,128)(2,1)S(1)}, u32[]{:S(2)}, u32[]{:S(2)}) collective-permute-start(bf16[64,512]{1,0:T(8,128)(2,1)S(1)} %get-tuple-element.18), channel_id=1, source_target_pairs={{0,128},{64,192},{128,0},{192,64},{256,384},{320,448},{384,256},{4... | collective-permute-start | bytes 196616 | tf_op jit(solution)/shard_map/ppermute | solution.py:254
  43.7 3.0 %collective-permute-start.2 = (bf16[64,512]{1,0:T(8,128)(2,1)S(1)}, bf16[64,512]{1,0:T(8,128)(2,1)S(1)}, u32[]{:S(2)}, u32[]{:S(2)}) collective-permute-start(bf16[64,512]{1,0:T(8,128)(2,1)S(1)} %get-tuple-element.19), channel_id=1, source_target_pairs={{0,192},{64,0},{128,64},{192,128},{256,448},{320,256},{384,320},{4... | collective-permute-start | bytes 196616 | tf_op jit(solution)/shard_map/ppermute | solution.py:254
  46.7 2.2 %collective-permute-done.2 = bf16[64,512]{1,0:T(8,128)(2,1)S(1)} collective-permute-done((bf16[64,512]{1,0:T(8,128)(2,1)S(1)}, bf16[64,512]{1,0:T(8,128)(2,1)S(1)}, u32[]{:S(2)}, u32[]{:S(2)}) %collective-permute-start.2) | collective-permute-done | bytes 65568 | tf_op jit(solution)/shard_map/ppermute | solution.py:254
  49.0 4.4 %collective-permute-start.5 = (bf16[256,512]{1,0:T(8,128)(2,1)S(1)}, bf16[256,512]{1,0:T(8,128)(2,1)S(1)}, u32[]{:S(2)}, u32[]{:S(2)}) collective-permute-start(bf16[256,512]{1,0:T(8,128)(2,1)S(1)} %constant_dynamic-update-slice_fusion.refs_0_), channel_id=1, source_target_pairs={{0,768},{64,832},{128,896},{192,960},{256,0},{320,64},{384,128},{4... | collective-permute-start | bytes 786440 | tf_op jit(solution)/shard_map/ppermute | solution.py:261
  53.4 2.4 %collective-permute-start.4 = (bf16[256,512]{1,0:T(8,128)(2,1)S(1)}, bf16[256,512]{1,0:T(8,128)(2,1)S(1)}, u32[]{:S(2)}, u32[]{:S(2)}) collective-permute-start(bf16[256,512]{1,0:T(8,128)(2,1)S(1)} %constant_dynamic-update-slice_fusion.refs_0_), channel_id=1, source_target_pairs={{0,512},{64,576},{128,640},{192,704},{256,768},{320,832},{384,896}... | collective-permute-start | bytes 786440 | tf_op jit(solution)/shard_map/ppermute | solution.py:261
  55.8 2.5 %collective-permute-start.3 = (bf16[256,512]{1,0:T(8,128)(2,1)S(1)}, bf16[256,512]{1,0:T(8,128)(2,1)S(1)}, u32[]{:S(2)}, u32[]{:S(2)}) collective-permute-start(bf16[256,512]{1,0:T(8,128)(2,1)S(1)} %constant_dynamic-update-slice_fusion.refs_0_), channel_id=1, source_target_pairs={{0,256},{64,320},{128,384},{192,448},{256,512},{320,576},{384,640}... | collective-permute-start | bytes 786440 | tf_op jit(solution)/shard_map/ppermute | solution.py:261
  58.4 0.1 select_reduce_fusion.band_ref
  58.6 4.1 %collective-permute-done.4.refs_2_ = bf16[256,512]{1,0:T(8,128)(2,1)S(1)} collective-permute-done((bf16[256,512]{1,0:T(8,128)(2,1)S(1)}, bf16[256,512]{1,0:T(8,128)(2,1)S(1)}, u32[]{:S(2)}, u32[]{:S(2)}) %collective-permute-start.4) | collective-permute-done | bytes 262176 | tf_op jit(solution)/shard_map/ppermute | solution.py:261
  62.7 7.2 %collective-permute-done.3.refs_1_ = bf16[256,512]{1,0:T(8,128)(2,1)S(1)} collective-permute-done((bf16[256,512]{1,0:T(8,128)(2,1)S(1)}, bf16[256,512]{1,0:T(8,128)(2,1)S(1)}, u32[]{:S(2)}, u32[]{:S(2)}) %collective-permute-start.3) | collective-permute-done | bytes 262176 | tf_op jit(solution)/shard_map/ppermute | solution.py:261
  69.9 1.4 shard_map.104
  71.3 15.1 %all_to_all.20.arrived_ref = bf16[16,40,512]{2,1,0:T(8,128)(2,1)S(1)} all-to-all(bf16[16,40,512]{2,1,0:T(8,128)(2,1)S(1)} %get-tuple-element.20), channel_id=1, replica_groups=mesh['dp'=16,'fsdp'=64] {'dp'}, dimensions={0} | all-to-all | bytes 1310720 | tf_op jit(solution)/shard_map/all_to_all | solution.py:273
  86.3 1.4 shard_map.105
  87.7 7.6 %all_to_all.21.back_ref = bf16[4,32,512]{2,1,0:T(8,128)(2,1)S(1)} all-to-all(bf16[4,32,512]{2,1,0:T(8,128)(2,1)S(1)} %shard_map.105), channel_id=1, replica_groups={{0,64,128,192},{256,320,384,448},{512,576,640,704},{768,832,896,960},{1..., dimensions={0} | all-to-all | bytes 262144 | tf_op jit(solution)/shard_map/all_to_all | solution.py:286
  95.3 1.3 shard_map.106._
  96.6 26.1 %all-to-all-start.3 = ((bf16[64,4,512]{2,1,0:T(4,128)(2,1)}), bf16[64,4,512]{2,1,0:T(4,128)(2,1)S(1)}, u32[]{:S(2)}, u32[]{:S(2)}) async-start(bf16[64,4,512]{2,1,0:T(4,128)(2,1)} %shard_map.106._), calls=%async_computation.3 | async-start | bytes 524288 | tf_op jit(solution)/shard_map/all_to_all | solution.py:50
  122.8 1.1 shard_map.108
  123.9 2.2 %collective-permute-start.6 = (bf16[64,512]{1,0:T(8,128)(2,1)S(1)}, bf16[64,512]{1,0:T(8,128)(2,1)S(1)}, u32[]{:S(2)}, u32[]{:S(2)}) collective-permute-start(bf16[64,512]{1,0:T(8,128)(2,1)S(1)} %get-tuple-element.22), channel_id=1, source_target_pairs={{0,64},{64,128},{128,192},{192,0},{256,320},{320,384},{384,448},{4... | collective-permute-start | bytes 196616 | tf_op jit(solution)/shard_map/ppermute | solution.py:254
  126.1 3.7 %collective-permute-start.7 = (bf16[64,512]{1,0:T(8,128)(2,1)S(1)}, bf16[64,512]{1,0:T(8,128)(2,1)S(1)}, u32[]{:S(2)}, u32[]{:S(2)}) collective-permute-start(bf16[64,512]{1,0:T(8,128)(2,1)S(1)} %get-tuple-element.23), channel_id=1, source_target_pairs={{0,128},{64,192},{128,0},{192,64},{256,384},{320,448},{384,256},{4... | collective-permute-start | bytes 196616 | tf_op jit(solution)/shard_map/ppermute | solution.py:254
  129.8 2.5 %collective-permute-start.8 = (bf16[64,512]{1,0:T(8,128)(2,1)S(1)}, bf16[64,512]{1,0:T(8,128)(2,1)S(1)}, u32[]{:S(2)}, u32[]{:S(2)}) collective-permute-start(bf16[64,512]{1,0:T(8,128)(2,1)S(1)} %get-tuple-element.24), channel_id=1, source_target_pairs={{0,192},{64,0},{128,64},{192,128},{256,448},{320,256},{384,320},{4... | collective-permute-start | bytes 196616 | tf_op jit(solution)/shard_map/ppermute | solution.py:254
  132.3 0.6 collective-permute-done.7.refs_2_
  132.9 2.2 %collective-permute-done.8.refs_3_ = bf16[64,512]{1,0:T(8,128)(2,1)S(1)} collective-permute-done((bf16[64,512]{1,0:T(8,128)(2,1)S(1)}, bf16[64,512]{1,0:T(8,128)(2,1)S(1)}, u32[]{:S(2)}, u32[]{:S(2)}) %collective-permute-start.8) | collective-permute-done | bytes 65568 | tf_op jit(solution)/shard_map/ppermute | solution.py:254
  135.1 0.9 shard_map.109
  136.0 9.6 %all-to-all-done.3.returned_ref = bf16[64,4,512]{2,1,0:T(4,128)(2,1)S(1)} async-done(((bf16[64,4,512]{2,1,0:T(4,128)(2,1)}), bf16[64,4,512]{2,1,0:T(4,128)(2,1)S(1)}, u32[]{:S(2)}, u32[]{:S(2)}) %all-to-all-start.3) | async-done | bytes 262176 | tf_op jit(solution)/shard_map/all_to_all | solution.py:50
  145.6 1.3 shard_map.107
  (26 shorter events, 0.3 us)
Async XLA Ops:
  0.6 0.7 copy-start.4
  1.3 0.9 copy-start.3
  3.6 31.0 %copy-start.5 = (bf16[1,4,8,1,4,512]{5,4,3,2,1,0:T(4,128)(2,1)S(1)}, bf16[1,4,8,1,4,512]{5,4,3,2,1,0:T(4,128)(2,1)}, u32[]{:S(2)}) copy-start(bf16[1,4,8,1,4,512]{5,4,3,2,1,0:T(4,128)(2,1)} %param.11) | copy-start | bytes 393220
  3.6 66.3 %all-to-all-start = ((bf16[64,4,512]{2,1,0:T(4,128)(2,1)}), bf16[64,4,512]{2,1,0:T(4,128)(2,1)S(1)}, u32[]{:S(2)}, u32[]{:S(2)}) async-start(bf16[64,4,512]{2,1,0:T(4,128)(2,1)} %shard_map.102), calls=%async_computation | async-start | bytes 524288 | tf_op jit(solution)/shard_map/all_to_all | solution.py:50
  34.6 0.9 copy-start.6
  35.9 10.8 %collective-permute-start = (bf16[64,512]{1,0:T(8,128)(2,1)S(1)}, bf16[64,512]{1,0:T(8,128)(2,1)S(1)}, u32[]{:S(2)}, u32[]{:S(2)}) collective-permute-start(bf16[64,512]{1,0:T(8,128)(2,1)S(1)} %get-tuple-element.17), channel_id=1, source_target_pairs={{0,64},{64,128},{128,192},{192,0},{256,320},{320,384},{384,448},{4... | collective-permute-start | bytes 196616 | tf_op jit(solution)/shard_map/ppermute | solution.py:254
  39.1 7.6 %collective-permute-start.1 = (bf16[64,512]{1,0:T(8,128)(2,1)S(1)}, bf16[64,512]{1,0:T(8,128)(2,1)S(1)}, u32[]{:S(2)}, u32[]{:S(2)}) collective-permute-start(bf16[64,512]{1,0:T(8,128)(2,1)S(1)} %get-tuple-element.18), channel_id=1, source_target_pairs={{0,128},{64,192},{128,0},{192,64},{256,384},{320,448},{384,256},{4... | collective-permute-start | bytes 196616 | tf_op jit(solution)/shard_map/ppermute | solution.py:254
  43.7 5.3 %collective-permute-start.2 = (bf16[64,512]{1,0:T(8,128)(2,1)S(1)}, bf16[64,512]{1,0:T(8,128)(2,1)S(1)}, u32[]{:S(2)}, u32[]{:S(2)}) collective-permute-start(bf16[64,512]{1,0:T(8,128)(2,1)S(1)} %get-tuple-element.19), channel_id=1, source_target_pairs={{0,192},{64,0},{128,64},{192,128},{256,448},{320,256},{384,320},{4... | collective-permute-start | bytes 196616 | tf_op jit(solution)/shard_map/ppermute | solution.py:254
  46.7 23.2 %copy-start.2 = (f32[1,4,8,1,4,512]{5,4,3,2,1,0:T(4,128)S(1)}, f32[1,4,8,1,4,512]{5,4,3,2,1,0:T(4,128)}, u32[]{:S(2)}) copy-start(f32[1,4,8,1,4,512]{5,4,3,2,1,0:T(4,128)} %param.13) | copy-start | bytes 786436
  49.0 9.6 %collective-permute-start.5 = (bf16[256,512]{1,0:T(8,128)(2,1)S(1)}, bf16[256,512]{1,0:T(8,128)(2,1)S(1)}, u32[]{:S(2)}, u32[]{:S(2)}) collective-permute-start(bf16[256,512]{1,0:T(8,128)(2,1)S(1)} %constant_dynamic-update-slice_fusion.refs_0_), channel_id=1, source_target_pairs={{0,768},{64,832},{128,896},{192,960},{256,0},{320,64},{384,128},{4... | collective-permute-start | bytes 786440 | tf_op jit(solution)/shard_map/ppermute | solution.py:261
  53.4 9.3 %collective-permute-start.4 = (bf16[256,512]{1,0:T(8,128)(2,1)S(1)}, bf16[256,512]{1,0:T(8,128)(2,1)S(1)}, u32[]{:S(2)}, u32[]{:S(2)}) collective-permute-start(bf16[256,512]{1,0:T(8,128)(2,1)S(1)} %constant_dynamic-update-slice_fusion.refs_0_), channel_id=1, source_target_pairs={{0,512},{64,576},{128,640},{192,704},{256,768},{320,832},{384,896}... | collective-permute-start | bytes 786440 | tf_op jit(solution)/shard_map/ppermute | solution.py:261
  55.8 14.1 %collective-permute-start.3 = (bf16[256,512]{1,0:T(8,128)(2,1)S(1)}, bf16[256,512]{1,0:T(8,128)(2,1)S(1)}, u32[]{:S(2)}, u32[]{:S(2)}) collective-permute-start(bf16[256,512]{1,0:T(8,128)(2,1)S(1)} %constant_dynamic-update-slice_fusion.refs_0_), channel_id=1, source_target_pairs={{0,256},{64,320},{128,384},{192,448},{256,512},{320,576},{384,640}... | collective-permute-start | bytes 786440 | tf_op jit(solution)/shard_map/ppermute | solution.py:261
  96.6 48.9 %all-to-all-start.3 = ((bf16[64,4,512]{2,1,0:T(4,128)(2,1)}), bf16[64,4,512]{2,1,0:T(4,128)(2,1)S(1)}, u32[]{:S(2)}, u32[]{:S(2)}) async-start(bf16[64,4,512]{2,1,0:T(4,128)(2,1)} %shard_map.106._), calls=%async_computation.3 | async-start | bytes 524288 | tf_op jit(solution)/shard_map/all_to_all | solution.py:50
  122.8 12.3 %copy-start = (f32[1,4,8,1,4,512]{5,4,3,2,1,0:T(4,128)S(1)}, f32[1,4,8,1,4,512]{5,4,3,2,1,0:T(4,128)}, u32[]{:S(2)}) copy-start(f32[1,4,8,1,4,512]{5,4,3,2,1,0:T(4,128)} %param.9) | copy-start | bytes 786436
  122.8 12.3 %copy-start.1 = (f32[1,4,8,1,4,512]{5,4,3,2,1,0:T(4,128)S(1)}, f32[1,4,8,1,4,512]{5,4,3,2,1,0:T(4,128)}, u32[]{:S(2)}) copy-start(f32[1,4,8,1,4,512]{5,4,3,2,1,0:T(4,128)} %param.10) | copy-start | bytes 786436
  123.9 8.4 %collective-permute-start.6 = (bf16[64,512]{1,0:T(8,128)(2,1)S(1)}, bf16[64,512]{1,0:T(8,128)(2,1)S(1)}, u32[]{:S(2)}, u32[]{:S(2)}) collective-permute-start(bf16[64,512]{1,0:T(8,128)(2,1)S(1)} %get-tuple-element.22), channel_id=1, source_target_pairs={{0,64},{64,128},{128,192},{192,0},{256,320},{320,384},{384,448},{4... | collective-permute-start | bytes 196616 | tf_op jit(solution)/shard_map/ppermute | solution.py:254
  126.1 6.8 %collective-permute-start.7 = (bf16[64,512]{1,0:T(8,128)(2,1)S(1)}, bf16[64,512]{1,0:T(8,128)(2,1)S(1)}, u32[]{:S(2)}, u32[]{:S(2)}) collective-permute-start(bf16[64,512]{1,0:T(8,128)(2,1)S(1)} %get-tuple-element.23), channel_id=1, source_target_pairs={{0,128},{64,192},{128,0},{192,64},{256,384},{320,448},{384,256},{4... | collective-permute-start | bytes 196616 | tf_op jit(solution)/shard_map/ppermute | solution.py:254
  129.8 5.3 %collective-permute-start.8 = (bf16[64,512]{1,0:T(8,128)(2,1)S(1)}, bf16[64,512]{1,0:T(8,128)(2,1)S(1)}, u32[]{:S(2)}, u32[]{:S(2)}) collective-permute-start(bf16[64,512]{1,0:T(8,128)(2,1)S(1)} %get-tuple-element.24), channel_id=1, source_target_pairs={{0,192},{64,0},{128,64},{192,128},{256,448},{320,256},{384,320},{4... | collective-permute-start | bytes 196616 | tf_op jit(solution)/shard_map/ppermute | solution.py:254
